TPU v7x, 32 devices: a whole 2x2x4 slice. The times are simulated.
32 devices in a mesh: seq: 8 (over z, x), batch: 4 (over y, core).
Axes of the slice: x: 2, y: 2, z: 4, core: 2. Of those that a mesh axis runs over, the one named last changes fastest.
Arguments:
- tokens: bfloat16 [4, 1024, 2048], P('batch', 'seq'), may hold values from -6 to 6
- modality: int32 [4, 1024], P('batch', 'seq'), may hold values from 0 to 2, as said below
- cotangent: bfloat16 [4, 1024, 2048], P('batch', 'seq'), may hold values from -6 to 6
- in_weight: float32 [2048, 3, 8192], P(('seq', 'batch')), may hold values from -0.125 to 0.125
- x_weight: float32 [4096, 3, 160], P(('seq', 'batch')), may hold values from -0.09375 to 0.09375
- dt_weight: float32 [4096, 3, 128], P(('seq', 'batch')), may hold values from -0.5 to 0.5
- out_weight: float32 [4096, 3, 2048], P(('seq', 'batch')), may hold values from -0.046875 to 0.046875
- norm_gain: float32 [2048, 3], P(('seq', 'batch')), may hold values from 0.5 to 1.5
- channel_params: float32 [4096, 25], P(('seq', 'batch'))
- in_first: float32 [2048, 3, 8192], P(('seq', 'batch')), may hold values from -112 to 112
- in_second: float32 [2048, 3, 8192], P(('seq', 'batch')), may hold values from 113 to 455
- x_first: float32 [4096, 3, 160], P(('seq', 'batch')), may hold values from -640 to 640
- x_second: float32 [4096, 3, 160], P(('seq', 'batch')), may hold values from 4095 to 16380
- dt_first: float32 [4096, 3, 128], P(('seq', 'batch')), may hold values from -64 to 64
- dt_second: float32 [4096, 3, 128], P(('seq', 'batch')), may hold values from 41 to 170
- out_first: float32 [4096, 3, 2048], P(('seq', 'batch')), may hold values from -320 to 320
- out_second: float32 [4096, 3, 2048], P(('seq', 'batch')), may hold values from 1023 to 4095
- gain_first: float32 [2048, 3], P(('seq', 'batch')), may hold values from -224 to 224
- gain_second: float32 [2048, 3], P(('seq', 'batch')), may hold values from 455 to 1820
- chan_first: float32 [4096, 25], P(('seq', 'batch')), may hold values from -640 to 640
- chan_second: float32 [4096, 25], P(('seq', 'batch')), may hold values from 4095 to 16380
Outputs:
- block_out: bfloat16 [4, 1024, 2048], P('batch', 'seq')
- input_grad: bfloat16 [4, 1024, 2048], P('batch', 'seq')
- in_weight_new: float32 [2048, 3, 8192], P(('seq', 'batch'))
- in_first_new: float32 [2048, 3, 8192], P(('seq', 'batch'))
- in_second_new: float32 [2048, 3, 8192], P(('seq', 'batch'))
- in_weight_low: bfloat16 [2048, 3, 8192], P(('seq', 'batch'))
- x_weight_new: float32 [4096, 3, 160], P(('seq', 'batch'))
- x_first_new: float32 [4096, 3, 160], P(('seq', 'batch'))
- x_second_new: float32 [4096, 3, 160], P(('seq', 'batch'))
- x_weight_low: bfloat16 [4096, 3, 160], P(('seq', 'batch'))
- dt_weight_new: float32 [4096, 3, 128], P(('seq', 'batch'))
- dt_first_new: float32 [4096, 3, 128], P(('seq', 'batch'))
- dt_second_new: float32 [4096, 3, 128], P(('seq', 'batch'))
- dt_weight_low: bfloat16 [4096, 3, 128], P(('seq', 'batch'))
- out_weight_new: float32 [4096, 3, 2048], P(('seq', 'batch'))
- out_first_new: float32 [4096, 3, 2048], P(('seq', 'batch'))
- out_second_new: float32 [4096, 3, 2048], P(('seq', 'batch'))
- out_weight_low: bfloat16 [4096, 3, 2048], P(('seq', 'batch'))
- gain_new: float32 [2048, 3], P(('seq', 'batch'))
- gain_first_new: float32 [2048, 3], P(('seq', 'batch'))
- gain_second_new: float32 [2048, 3], P(('seq', 'batch'))
- chan_new: float32 [4096, 25], P(('seq', 'batch'))
- chan_first_new: float32 [4096, 25], P(('seq', 'batch'))
- chan_second_new: float32 [4096, 25], P(('seq', 'batch'))
Inputs may be any that keep to these rules, and one draw needn't show every extreme that they name: modality is constant over each aligned run of 128 positions of a sequence.
All inputs are finite; a program needn't handle non-finite values.
Results may differ from a plain program's by a relative error of at most 0.014.
The roundings to bfloat16 on the way count: a program that leaves them out, or rounds other values in their place, can miss the bound.
Values may be sent and summed in bfloat16 or wider, within the bound.
A program may use at most 832 MiB of HBM per device.

v0:
```python
import jax
import jax.numpy as jnp
from jax import lax
from jax.sharding import PartitionSpec as P

D = 2048
INNER = 4096
STATE = 16
CONV = 4
RANK = 128
MODES = 3
MBLK = 128
SCAN_BLOCK = 32
STEP = 5


NORM_EPS = 1e-05
BETA_ONE = 0.5
BETA_TWO = 0.75
ADAM_EPS = 1e-08
DECAY = 0.01
SMALL_RATE = 0.1
CHAN_RATE = 2.0
HIGHEST = lax.Precision.HIGHEST


def passed_along(block, axis, distance):
    devices = range(lax.axis_size(axis))
    route = [(i - distance, i) for i in devices if i - distance in devices]
    return lax.ppermute(block, axis, route)


def carried_in(array, axis, combine, identity, reverse):
    count, mine = (lax.axis_size(axis), lax.axis_index(axis))
    everything = jax.tree.map(lambda part: lax.all_gather(part, axis), array)
    start = jax.tree.map(
        lambda part, zero: jnp.broadcast_to(jnp.asarray(zero, part.dtype), part.shape),
        array,
        identity,
    )

    def lap(k, before):
        at = count - 1 - k if reverse else k
        reached = at > mine if reverse else at < mine
        new = combine(before, jax.tree.map(lambda part: part[at], everything))
        return jax.tree.map(lambda a, b: jnp.where(reached, a, b), new, before)

    return lax.fori_loop(0, count, lap, start)


def combine_maps(earlier, later):
    return (earlier[0] * later[0], later[0] * earlier[1] + later[1])


def mode_product(left, weights, block_modes, block, flip):
    length = left.shape[0]
    pieces = left.reshape(length // block, block, left.shape[1])

    def one_block(pair):
        piece, mode = pair
        matrix = lax.dynamic_index_in_dim(weights, mode, 1, keepdims=False)
        if flip:
            return lax.dot_general(
                piece, matrix, (((1,), (1,)), ((), ())), preferred_element_type=jnp.float32
            )
        return jnp.dot(piece, matrix, preferred_element_type=jnp.float32)

    return lax.map(one_block, (pieces, block_modes)).reshape(length, -1)


def mode_grads(lefts, rights, block_modes, count, modes):
    width = sum((right.shape[1] for right in rights))
    initial = jnp.zeros((count, modes, width), jnp.float32)

    def add_block(j, total):
        parts = []
        for left, right in zip(lefts, rights):
            parts.append(
                lax.dot_general(
                    left, right, (((0,), (0,)), ((), ())), preferred_element_type=jnp.float32
                )
            )
        joined = jnp.concatenate(parts, 1)[:, None, :]
        mode = block_modes[j]
        before = lax.dynamic_slice_in_dim(total, mode, 1, 1)
        return lax.dynamic_update_slice_in_dim(total, before + joined, mode, 1)

    return lax.fori_loop(0, block_modes.shape[0], add_block, initial)


def scan_piece(carry, inputs, rates_t):
    steps, drives, entry, leave = inputs
    decay = jnp.exp(steps[:, None, :] * rates_t[None, :, :])
    push = drives[:, None, :] * entry[:, :, None]
    decay_all, push_all = lax.associative_scan(combine_maps, (decay, push), axis=0)
    states = decay_all * carry[None] + push_all
    return (states[-1], jnp.sum(states * leave[:, :, None], 1))


def local_scan(steps, drives, entry, leave, rates_t, start_state, block):
    length = steps.shape[0]
    count = length // block
    shaped = tuple(
        (part.reshape(count, block, part.shape[1]) for part in (steps, drives, entry, leave))
    )

    def piece_step(carry, inputs):
        return scan_piece(carry, inputs, rates_t)

    final, outs = lax.scan(jax.checkpoint(piece_step), start_state, shaped)
    return (final, outs.reshape(length, -1))


def start_gradient(steps, weighted, leave, rates_t, block):
    length = steps.shape[0]
    count = length // block
    totals = jnp.cumsum(steps, 0)
    shaped = (
        totals.reshape(count, block, -1),
        weighted.reshape(count, block, -1),
        leave.reshape(count, block, -1),
    )

    def add_piece(carry, inputs):
        sums, weights_now, leave_now = inputs
        decays = jnp.exp(sums[:, None, :] * rates_t[None, :, :])
        return (carry + jnp.sum(decays * weights_now[:, None, :] * leave_now[:, :, None], 0), None)

    result, _ = lax.scan(add_piece, jnp.zeros(rates_t.shape, jnp.float32), shaped)
    return result


def adam_update(weight, first, second, grad, rate):
    first_new = BETA_ONE * first + (1.0 - BETA_ONE) * grad
    second_new = BETA_TWO * second + (1.0 - BETA_TWO) * grad * grad
    first_hat = first_new / (1.0 - BETA_ONE**STEP)
    second_hat = second_new / (1.0 - BETA_TWO**STEP)
    weight_new = weight - rate * (first_hat / (jnp.sqrt(second_hat) + ADAM_EPS) + DECAY * weight)
    return (weight_new, first_new, second_new)


def body(
    tokens,
    modality,
    cotangent,
    in_weight,
    x_weight,
    dt_weight,
    out_weight,
    norm_gain,
    channel_params,
    in_first,
    in_second,
    x_first,
    x_second,
    dt_first,
    dt_second,
    out_first,
    out_second,
    gain_first,
    gain_second,
    chan_first,
    chan_second,
):
    x_rows = tokens[0].astype(jnp.float32)
    grad_out = cotangent[0]
    kinds = modality[0]
    length = x_rows.shape[0]
    block_modes = kinds[::MBLK]
    one_hot = (kinds[:, None] == jnp.arange(MODES, dtype=jnp.int32)[None, :]).astype(jnp.float32)
    shards = (
        in_weight.astype(jnp.bfloat16),
        x_weight.astype(jnp.bfloat16),
        dt_weight.astype(jnp.bfloat16),
        out_weight.astype(jnp.bfloat16),
        norm_gain.astype(jnp.bfloat16),
        channel_params.astype(jnp.bfloat16),
    )
    in_matrix, x_matrix, dt_matrix, out_matrix, gain_all, chan_all = (
        lax.all_gather(shards[0], ("seq", "batch"), axis=0, tiled=True),
        lax.all_gather(shards[1], ("seq", "batch"), axis=0, tiled=True),
        lax.all_gather(shards[2], ("seq", "batch"), axis=0, tiled=True),
        lax.all_gather(shards[3], ("seq", "batch"), axis=0, tiled=True),
        lax.all_gather(shards[4], ("seq", "batch"), axis=0, tiled=True),
        lax.all_gather(shards[5], ("seq", "batch"), axis=0, tiled=True),
    )
    gain_full = gain_all.astype(jnp.float32)
    chan_full = chan_all.astype(jnp.float32)
    step_bias = chan_full[:, :MODES]
    conv_bias = chan_full[:, MODES]
    skip = chan_full[:, MODES + 1]
    conv_taps = chan_full[:, MODES + 2 : MODES + 2 + CONV]
    log_rates = chan_full[:, MODES + 2 + CONV :]

    def normed(x_in, gain_in):
        scale = lax.rsqrt(jnp.mean(x_in * x_in, -1, keepdims=True) + NORM_EPS)
        return x_in * scale * jnp.dot(one_hot, gain_in.T, precision=HIGHEST)

    normal, norm_back = jax.vjp(normed, x_rows, gain_full)
    normal_low = normal.astype(jnp.bfloat16)
    joint = mode_product(normal_low, in_matrix, block_modes, MBLK, False)
    inner_low = joint[:, :INNER].astype(jnp.bfloat16)
    gate = joint[:, INNER:]
    borrowed = passed_along(inner_low[length - (CONV - 1) :], "seq", 1)
    extended = jnp.concatenate([borrowed, inner_low], 0).astype(jnp.float32)

    def convolve(wider, taps, bias):
        total = bias[None, :]
        for k in range(CONV):
            total = total + taps[:, k][None, :] * wider[k : k + length]
        return jax.nn.silu(total)

    act, conv_back = jax.vjp(convolve, extended, conv_taps, conv_bias)
    act_low = act.astype(jnp.bfloat16)
    act_full = act_low.astype(jnp.float32)
    projected = mode_product(act_low, x_matrix, block_modes, MBLK, False)
    rank_low = projected[:, :RANK].astype(jnp.bfloat16)
    entry = projected[:, RANK : RANK + STATE]
    leave = projected[:, RANK + STATE :]
    step_raw = mode_product(rank_low, dt_matrix, block_modes, MBLK, True)
    rates_t = -jnp.exp(log_rates).T
    steps = jax.nn.softplus(step_raw + jnp.dot(one_hot, step_bias.T, precision=HIGHEST))
    through = jnp.exp(rates_t * jnp.sum(steps, 0)[None, :])
    zero_state = jnp.zeros((STATE, INNER), jnp.float32)
    alone, _ = local_scan(steps, steps * act_full, entry, leave, rates_t, zero_state, SCAN_BLOCK)
    start_state = carried_in(
        (through, alone),
        "seq",
        combine_maps,
        (jnp.ones_like(through), jnp.zeros_like(alone)),
        False,
    )[1]

    def mixer(
        raw_steps, inner_act, entry_in, leave_in, gate_in, bias_in, log_in, skip_in, start_in
    ):
        rates_in = -jnp.exp(log_in).T
        steps_in = jax.nn.softplus(raw_steps + jnp.dot(one_hot, bias_in.T, precision=HIGHEST))
        final, outs = local_scan(
            steps_in, steps_in * inner_act, entry_in, leave_in, rates_in, start_in, SCAN_BLOCK
        )
        return ((outs + skip_in * inner_act) * jax.nn.silu(gate_in), final)

    (mixed, _), mixer_back = jax.vjp(
        mixer, step_raw, act_full, entry, leave, gate, step_bias, log_rates, skip, start_state
    )
    mixed_low = mixed.astype(jnp.bfloat16)
    result = x_rows + mode_product(mixed_low, out_matrix, block_modes, MBLK, False)
    block_out = result.astype(jnp.bfloat16)[None]
    x_back, dt_back, out_back = (
        lax.all_gather(shards[1], ("seq", "batch"), axis=0, tiled=True),
        lax.all_gather(shards[2], ("seq", "batch"), axis=0, tiled=True),
        lax.all_gather(shards[3], ("seq", "batch"), axis=0, tiled=True),
    )
    back_mixed = mode_product(grad_out, out_back, block_modes, MBLK, True)
    start_grad = start_gradient(steps, back_mixed * jax.nn.silu(gate), leave, rates_t, SCAN_BLOCK)
    end_grad = carried_in(
        (through, start_grad),
        "seq",
        combine_maps,
        (jnp.ones_like(through), jnp.zeros_like(start_grad)),
        True,
    )[1]
    grads = mixer_back((back_mixed, end_grad))
    back_raw, back_act, back_entry, back_leave, back_gate, back_bias, back_log, back_skip, _ = grads
    raw_low = back_raw.astype(jnp.bfloat16)
    back_rank = mode_product(raw_low, dt_back, block_modes, MBLK, False)
    back_proj_low = jnp.concatenate([back_rank, back_entry, back_leave], 1).astype(jnp.bfloat16)
    back_act_all = back_act + mode_product(back_proj_low, x_back, block_modes, MBLK, True)
    e_shard = lax.psum_scatter(
        mode_grads(
            (act_low, raw_low, mixed_low),
            (back_proj_low, rank_low, grad_out),
            block_modes,
            x_weight.shape[0] * lax.axis_size(("seq", "batch")),
            MODES,
        ),
        ("seq", "batch"),
        scatter_dimension=0,
        tiled=True,
    )
    x_grad = e_shard[:, :, : RANK + 2 * STATE]
    dt_grad = e_shard[:, :, RANK + 2 * STATE : 2 * RANK + 2 * STATE]
    out_grad = e_shard[:, :, 2 * RANK + 2 * STATE :]
    back_wide, back_taps, back_cbias = conv_back(back_act_all)
    from_next = passed_along(back_wide[: CONV - 1].astype(jnp.bfloat16), "seq", -1).astype(
        jnp.float32
    )
    back_inner = back_wide[CONV - 1 :]
    back_inner = jnp.concatenate(
        [back_inner[: length - (CONV - 1)], back_inner[length - (CONV - 1) :] + from_next], 0
    )
    joint_low = jnp.concatenate([back_inner, back_gate], 1).astype(jnp.bfloat16)
    back_normal = mode_product(
        joint_low,
        lax.all_gather(shards[0], ("seq", "batch"), axis=0, tiled=True),
        block_modes,
        MBLK,
        True,
    )
    band = lax.psum_scatter(
        mode_grads(
            (normal_low,),
            (joint_low,),
            block_modes,
            lax.axis_size("seq") * (in_weight.shape[0] * lax.axis_size("batch")),
            MODES,
        ).astype(jnp.bfloat16),
        "seq",
        scatter_dimension=0,
        tiled=True,
    ).astype(jnp.float32)
    in_grad = lax.psum_scatter(band, "batch", scatter_dimension=0, tiled=True)
    back_x, back_gain = norm_back(back_normal)
    input_grad = (grad_out.astype(jnp.float32) + back_x).astype(jnp.bfloat16)[None]
    back_chan = jnp.concatenate(
        [back_bias, back_cbias[:, None], back_skip[:, None], back_taps, back_log], 1
    )
    gain_grad, chan_grad = (
        lax.psum_scatter(back_gain, ("seq", "batch"), scatter_dimension=0, tiled=True),
        lax.psum_scatter(back_chan, ("seq", "batch"), scatter_dimension=0, tiled=True),
    )
    in_new = adam_update(in_weight, in_first, in_second, in_grad, D ** (-0.5))
    x_new = adam_update(x_weight, x_first, x_second, x_grad, INNER ** (-0.5))
    dt_new = adam_update(dt_weight, dt_first, dt_second, dt_grad, RANK ** (-0.5))
    out_new = adam_update(out_weight, out_first, out_second, out_grad, (4 * INNER) ** (-0.5))
    gain_new = adam_update(norm_gain, gain_first, gain_second, gain_grad, SMALL_RATE)
    chan_new = adam_update(channel_params, chan_first, chan_second, chan_grad, CHAN_RATE)
    return (
        block_out,
        input_grad,
        in_new[0],
        in_new[1],
        in_new[2],
        in_new[0].astype(jnp.bfloat16),
        x_new[0],
        x_new[1],
        x_new[2],
        x_new[0].astype(jnp.bfloat16),
        dt_new[0],
        dt_new[1],
        dt_new[2],
        dt_new[0].astype(jnp.bfloat16),
        out_new[0],
        out_new[1],
        out_new[2],
        out_new[0].astype(jnp.bfloat16),
        gain_new[0],
        gain_new[1],
        gain_new[2],
        chan_new[0],
        chan_new[1],
        chan_new[2],
    )


def solution(mesh):
    placed = (
        P("batch", "seq", None),
        P("batch", "seq"),
        P("batch", "seq", None),
        P(("seq", "batch"), None, None),
        P(("seq", "batch"), None, None),
        P(("seq", "batch"), None, None),
        P(("seq", "batch"), None, None),
        P(("seq", "batch"), None),
        P(("seq", "batch"), None),
        P(("seq", "batch"), None, None),
        P(("seq", "batch"), None, None),
        P(("seq", "batch"), None, None),
        P(("seq", "batch"), None, None),
        P(("seq", "batch"), None, None),
        P(("seq", "batch"), None, None),
        P(("seq", "batch"), None, None),
        P(("seq", "batch"), None, None),
        P(("seq", "batch"), None),
        P(("seq", "batch"), None),
        P(("seq", "batch"), None),
        P(("seq", "batch"), None),
    )
    return jax.shard_map(
        body,
        mesh=mesh,
        in_specs=placed,
        out_specs=(
            P("batch", "seq", None),
            P("batch", "seq", None),
            P(("seq", "batch"), None, None),
            P(("seq", "batch"), None, None),
            P(("seq", "batch"), None, None),
            P(("seq", "batch"), None, None),
            P(("seq", "batch"), None, None),
            P(("seq", "batch"), None, None),
            P(("seq", "batch"), None, None),
            P(("seq", "batch"), None, None),
            P(("seq", "batch"), None, None),
            P(("seq", "batch"), None, None),
            P(("seq", "batch"), None, None),
            P(("seq", "batch"), None, None),
            P(("seq", "batch"), None, None),
            P(("seq", "batch"), None, None),
            P(("seq", "batch"), None, None),
            P(("seq", "batch"), None, None),
            P(("seq", "batch"), None),
            P(("seq", "batch"), None),
            P(("seq", "batch"), None),
            P(("seq", "batch"), None),
            P(("seq", "batch"), None),
            P(("seq", "batch"), None),
        ),
        check_vma=False,
    )
```

profile of v0, /device:TPU:10, one launch (start us, length us, event | category | flops | bytes accessed | tf_op | source)
XLA Modules:
  0.0 7653.1 jit_solution(5292888772615738180)
XLA Ops:
  19.1 32.0 all-gather.3
  51.3 43.5 all_gather.42
  97.7 432.1 %all-gather.12.cloned.1.call-done = bf16[2048,3,8192]{2,0,1:T(8,128)(2,1)} async-done(((bf16[64,3,8192]{2,0,1:T(8,128)(2,1)}), bf16[2048,3,8192]{2,0,1:T(8,128)(2,1)}) %all-gather.12.cloned.1.call-update) | async-done | bytes 100663312 | tf_op jit(solution)/shard_map/all_gather | solution.py:180
  554.4 252.8 %all-gather.18.cloned.1.call-done = bf16[4096,3,2048]{2,0,1:T(8,128)(2,1)} async-done(((bf16[128,3,2048]{2,0,1:T(8,128)(2,1)}), bf16[4096,3,2048]{2,0,1:T(8,128)(2,1)}) %all-gather.18.cloned.1.call-update) | async-done | bytes 50331664 | tf_op jit(solution)/shard_map/all_gather | solution.py:183
  807.1 17.7 fusion.59
  824.8 47.9 all-gather.14.cloned.1.call-done
  874.6 60.3 all-gather.16.cloned.1.call-done
  962.4 613.7 %while.26 = (s32[]{:T(128)}, f32[16,4096]{1,0:T(8,128)}, f32[4,32,4096]{2,1,0:T(8,128)}, f32[16,4096]{1,0:T(8,128)S(1)}, f32[4,32,4096]{2,1,0:T(8,128)}, /*index=5*/f32[4,32,16]{1,2,0:T(8,128)S(1)}, s32[]{:T(128)}, f32[]{:T(128)}) while((s32[]{:T(128)}, f32[16,4096]{1,0:T(8,128)}, f32[4,32,4096]{2,1,0:T(8,128)}, f32[16,4096]{1,0:T(8,128)S(1)}, ...), condition=%wide.region_3.4_spmd, body=%wide.region_2.3_spmd.sunk | while | flops 19922944 | bytes 287582624 | solution.py:110
  1591.0 34.0 all-gather.22.cloned.1.call-done
  1641.4 873.3 %while.27 = (s32[]{:T(128)}, f32[16,4096]{1,0:T(8,128)}, f32[4,32,4096]{2,1,0:T(8,128)}, f32[4,16,4096]{2,1,0:T(8,128)}, f32[4,32,4096]{2,1,0:T(8,128)}, /*index...) while((s32[]{:T(128)}, f32[16,4096]{1,0:T(8,128)}, ...), condition=%wide.region_8.9_spmd, body=%wide.region_6.8_spmd.sunk | while | flops 39124992 | bytes 406344192 | solution.py:110
  2519.1 2132.2 %while.62 = (s32[]{:T(128)}, f32[16,4096]{1,0:T(8,128)}, f32[16,4096]{1,0:T(8,128)}, f32[4,32,4096]{2,1,0:T(8,128)}, f32[4,32,4096]{2,1,0:T(8,128)}, /*index=5*/...) while((s32[]{:T(128)}, f32[16,4096]{1,0:T(8,128)}, ...), condition=%wide.region_22.23_spmd.clone, body=%wide.region_15.22_spmd.clone.sunk | while | flops 123337728 | bytes 1199649536 | solution.py:110
  2696.8 20.2 slice_multiply_fusion.69
  3222.5 20.2 slice_multiply_fusion.69
  3748.1 20.2 slice_multiply_fusion.69
  4273.7 20.2 slice_multiply_fusion.69
  4675.5 31.1 broadcast_in_dim.159
  4740.6 18.5 fusion.79
  4768.5 37.1 broadcast_in_dim.161
  4805.6 24.7 fusion.24
  4830.4 1425.0 %reduce-scatter.8.cloned.1.call-done = bf16[256,3,8192]{2,0,1:T(8,128)(2,1)} async-done(((bf16[2048,3,8192]{2,0,1:T(8,128)(2,1)}), bf16[256,3,8192]{2,0,1:T(8,128)(2,1)}) %reduce-scatter.8.cloned.1.call-update) | async-done | bytes 12582928 | tf_op jit(solution)/shard_map/reduce_scatter | solution.py:301
  6294.7 70.6 reduce-scatter.16.cloned.1.call-done
  6368.1 129.8 %reduce-scatter.14.cloned.1.call-done = f32[128,25]{0,1:T(8,128)} async-done(((f32[4096,25]{0,1:T(8,128)}), f32[128,25]{0,1:T(8,128)}) %reduce-scatter.14.cloned.1.call-update) | async-done | bytes 12816 | tf_op jit(solution)/shard_map/reduce_scatter | solution.py:321
  6499.2 948.0 %reduce-scatter.12.cloned.1.call-done = f32[128,3,2336]{0,2,1:T(8,128)} async-done(((f32[4096,3,2336]{0,2,1:T(8,128)}), f32[128,3,2336]{0,2,1:T(8,128)}) %reduce-scatter.12.cloned.1.call-update) | async-done | bytes 3588112 | tf_op jit(solution)/shard_map/reduce_scatter | solution.py:270
  7483.8 146.8 %reduce-scatter.10.cloned.1.call-done = f32[64,3,8192]{2,0,1:T(8,128)} async-done(((f32[256,3,8192]{2,0,1:T(8,128)}), f32[64,3,8192]{2,0,1:T(8,128)}) %reduce-scatter.10.cloned.1.call-update) | async-done | bytes 6291472 | tf_op jit(solution)/shard_map/reduce_scatter | solution.py:313
  (1901 shorter events, 3803.0 us)
Async XLA Ops:
  7.2 522.6 %all-gather.12.cloned.1.call-start = ((), (), s32[]{:S(2)}) async-start(), calls=%async_computation.5 | async-start | bytes 103809024 | tf_op jit(solution)/shard_map/all_gather | solution.py:180
  12.2 795.0 %all-gather.18.cloned.1.call-start = ((), (), s32[]{:S(2)}) async-start(), calls=%async_computation.8 | async-start | bytes 51904512 | tf_op jit(solution)/shard_map/all_gather | solution.py:183
  15.4 857.4 %all-gather.14.cloned.1.call-start = ((), (), s32[]{:S(2)}) async-start(), calls=%async_computation.6 | async-start | bytes 4055040 | tf_op jit(solution)/shard_map/all_gather | solution.py:181
  16.1 918.8 %all-gather.16.cloned.1.call-start = ((), (), s32[]{:S(2)}) async-start(), calls=%async_computation.7 | async-start | bytes 3244032 | tf_op jit(solution)/shard_map/all_gather | solution.py:182
  17.8 1558.4 %all-gather.20.cloned.1.call-start = ((), (), s32[]{:S(2)}) async-start(), calls=%async_computation.13 | async-start | bytes 2359296 | tf_op jit(solution)/shard_map/all_gather | solution.py:35
  19.1 525.7 %copy-start.142 = (f32[128]{0:T(128)}, f32[128]{0:T(128)S(1)}, u32[]{:S(2)}) copy-start(f32[128]{0:T(128)S(1)} %fusion.78) | copy-start | bytes 1540
  94.8 434.9 %copy-start.101 = (f32[4096,25]{0,1:T(8,128)}, f32[4096,25]{0,1:T(8,128)S(1)}, u32[]{:S(2)}) copy-start(f32[4096,25]{0,1:T(8,128)S(1)} %convert_element_type.88) | copy-start | bytes 1228804
  95.5 434.3 %copy-start.139 = (f32[128]{0:T(128)}, f32[128]{0:T(128)S(1)}, u32[]{:S(2)}) copy-start(f32[128]{0:T(128)S(1)} %fusion.117) | copy-start | bytes 1540
  96.8 447.9 %copy-start.90 = (bf16[128,2048]{1,0:T(8,128)(2,1)}, bf16[128,2048]{1,0:T(8,128)(2,1)S(1)}, u32[]{:S(2)}) copy-start(bf16[128,2048]{1,0:T(8,128)(2,1)S(1)} %get-tuple-element.1518) | copy-start | bytes 1572868
  544.8 7.9 collective-permute-start
  551.3 273.5 %copy-start.122 = (f32[4096,1]{0,1:T(1,128)}, f32[4096,1]{0,1:T(1,128)S(1)}, u32[]{:S(2)}) copy-start(f32[4096,1]{0,1:T(1,128)S(1)} %get-tuple-element.1510) | copy-start | bytes 49156
  551.3 273.5 %copy-start.124 = (f32[4096,1]{0,1:T(1,128)}, f32[4096,1]{0,1:T(1,128)S(1)}, u32[]{:S(2)}) copy-start(f32[4096,1]{0,1:T(1,128)S(1)} %get-tuple-element.1511) | copy-start | bytes 49156
  551.3 273.5 %copy-start.126 = (f32[4096,1]{0,1:T(1,128)}, f32[4096,1]{0,1:T(1,128)S(1)}, u32[]{:S(2)}) copy-start(f32[4096,1]{0,1:T(1,128)S(1)} %get-tuple-element.1512) | copy-start | bytes 49156
  551.3 273.5 %copy-start.128 = (f32[4096,1]{0,1:T(1,128)}, f32[4096,1]{0,1:T(1,128)S(1)}, u32[]{:S(2)}) copy-start(f32[4096,1]{0,1:T(1,128)S(1)} %get-tuple-element.1513) | copy-start | bytes 49156
  942.7 633.5 %all-gather.24.cloned.1.call-start = ((), (), s32[]{:S(2)}) async-start(), calls=%async_computation.15 | async-start | bytes 2359296 | tf_op jit(solution)/shard_map/all_gather | solution.py:35
  961.6 663.5 %all-gather.22.cloned.1.call-start = ((), (), s32[]{:S(2)}) async-start(), calls=%async_computation.14 | async-start | bytes 2359296 | tf_op jit(solution)/shard_map/all_gather | solution.py:35
  1576.1 4679.3 %reduce-scatter.8.cloned.1.call-start = ((), (), s32[]{:S(2)}) async-start(), calls=%async_computation.9 | async-start | bytes 113246208 | tf_op jit(solution)/shard_map/reduce_scatter | solution.py:301
  4668.8 6.7 collective-permute-start.1
  4720.4 1644.9 %reduce-scatter.16.cloned.1.call-start = ((), (), s32[]{:S(2)}) async-start(), calls=%async_computation.16 | async-start | bytes 1081344
  4762.4 1735.4 %reduce-scatter.14.cloned.1.call-start = ((), (), s32[]{:S(2)}) async-start(), calls=%async_computation.12 | async-start | bytes 540672 | tf_op jit(solution)/shard_map/reduce_scatter | solution.py:321
  4768.4 2678.8 %reduce-scatter.12.cloned.1.call-start = ((), (), s32[]{:S(2)}) async-start(), calls=%async_computation.11 | async-start | bytes 118407168 | tf_op jit(solution)/shard_map/reduce_scatter | solution.py:270
  4830.4 2800.2 %reduce-scatter.10.cloned.1.call-start = ((), (), s32[]{:S(2)}) async-start(), calls=%async_computation.10 | async-start | bytes 31457280 | tf_op jit(solution)/shard_map/reduce_scatter | solution.py:313
  6293.4 204.4 %copy-start.118 = (f32[128,25]{0,1:T(8,128)S(1)}, f32[128,25]{0,1:T(8,128)}, u32[]{:S(2)}) copy-start(f32[128,25]{0,1:T(8,128)} %param.41) | copy-start | bytes 38404
  6293.5 1162.6 %copy-start.77 = (f32[128,3,2048]{0,2,1:T(8,128)S(1)}, f32[128,3,2048]{0,2,1:T(8,128)}, u32[]{:S(2)}) copy-start(f32[128,3,2048]{0,2,1:T(8,128)} %copy.148) | copy-start | bytes 9437188
  (415 other events, 3405.8 us)
Sparse Core Ops, SparseCore 0:
  12.2 517.4 all-gather.11
  533.3 273.8 all-gather.17
  810.6 62.1 all-gather.13
  876.1 58.7 all-gather.15
  942.8 48.7 all-gather.19
  993.6 47.7 all-gather.23
  1576.2 48.7 all-gather.21
  4720.5 1534.8 reduce-scatter.7
  6258.3 106.9 reduce-scatter.15
  6368.0 129.8 reduce-scatter.13
  6505.4 941.7 reduce-scatter.11
  7449.7 180.8 reduce-scatter.9
where the time goes:
time: 7700 us; the launch traced here: 7650 us
  waiting for transfers between devices  3550 us (46%)
  local copies, waits for them, and re-layouts  2230 us (29%)
  other arithmetic  1610 us (21%)
  matrix products  113 us (1%)
    pad x296, local copies, waits for them, and re-layouts, scan_piece(): lax.associative_scan(combine_maps, (decay, push), axis=0)  1760 us
    reduce_scatter x1, waiting for transfers between devices, body(): lax.psum_scatter(mode_grads((normal_low,), (joint_low,), block_modes, lax...  1420 us
    reduce_scatter x1, waiting for transfers between devices, body(): lax.psum_scatter(mode_grads((act_low, raw_low, mixed_low), (back_proj_low...  948 us
    mul x104, other arithmetic, combine_maps(): return (earlier[0] * later[0], later[0] * earlier[1] + later[1])  495 us
    all_gather x1, waiting for transfers between devices, body(): lax.all_gather(shards[0], ('seq', 'batch'), axis=0, tiled=True)  432 us
    add x96, other arithmetic, scan_piece(): lax.associative_scan(combine_maps, (decay, push), axis=0)  291 us
    all_gather x1, waiting for transfers between devices, body(): lax.all_gather(shards[3], ('seq', 'batch'), axis=0, tiled=True)  253 us
    while x648, local copies, waits for them, and re-layouts  194 us
  transfers between devices with their start and end apart: 14, of which 11 were waited for; matrix products, arithmetic and copies ran while one was open for 11% of the time, Pallas kernels for 0%

commit v1 on v0

v1 whole, which is shorter than its diff:
```python
import functools

import jax
import jax.numpy as jnp
import numpy as np
from jax import lax
from jax.experimental import pallas as pl
from jax.experimental.pallas import tpu as pltpu
from jax.sharding import Mesh
from jax.sharding import PartitionSpec as P

D = 2048
INNER = 4096
STATE = 16
CONV = 4
RANK = 128
MODES = 3
MBLK = 128
STEP = 5
XCOLS = RANK + 2 * STATE
GROUPS = 16

NORM_EPS = 1e-05
BETA_ONE = 0.5
BETA_TWO = 0.75
ADAM_EPS = 1e-08
DECAY = 0.01
SMALL_RATE = 0.1
CHAN_RATE = 2.0
LN2 = 0.6931471805599453
F32 = jnp.float32
BF16 = jnp.bfloat16

EVERY = ("seq", "hi", "lo")
GROUP = ("seq", "hi")
VMEM = pltpu.VMEM
MIB = 1024 * 1024


def adam_update(weight, first, second, grad, rate):
    first_new = BETA_ONE * first + (1.0 - BETA_ONE) * grad
    second_new = BETA_TWO * second + (1.0 - BETA_TWO) * grad * grad
    first_hat = first_new / (1.0 - BETA_ONE**STEP)
    second_hat = second_new / (1.0 - BETA_TWO**STEP)
    weight_new = weight - rate * (first_hat / (jnp.sqrt(second_hat) + ADAM_EPS) + DECAY * weight)
    return (weight_new, first_new, second_new)


def nt_dot(left, right):
    return lax.dot_general(left, right, (((1,), (1,)), ((), ())), preferred_element_type=F32)


def tn_dot(left, right):
    return lax.dot_general(left, right, (((0,), (0,)), ((), ())), preferred_element_type=F32)


def nn_dot(left, right):
    return jnp.dot(left, right, preferred_element_type=F32)


def add_outer(total_ref, mode, x_ref, q, right):
    piece = 512
    for k in range(D // piece):
        at = slice(k * piece, (k + 1) * piece)
        total_ref[mode, at, :] += tn_dot(x_ref[q, :, at], right)


def sigmoid(v):
    return 1.0 / (1.0 + jnp.exp(-v))


def rounded(v):
    return lax.reduce_precision(v, 8, 7)


def softplus(v):
    return jnp.maximum(v, 0.0) + jnp.log1p(jnp.exp(-jnp.abs(v)))


class Plan:
    def __init__(self, blocks, seqs, channels):
        self.nb = blocks
        self.seqs = seqs
        self.chan = channels
        self.halves = channels // 128
        self.fold = 8 // self.seqs
        self.groups = STATE // self.fold
        self.held = self.groups * self.halves

    def sub(self, f, q):
        return f * self.seqs + q

    def select(self):
        out = np.zeros((self.fold, 2 * STATE, 128), np.float32)
        for f in range(self.fold):
            for g in range(self.groups):
                out[f, g * self.fold + f, g] = 1.0
                out[f, STATE + g * self.fold + f, self.groups + g] = 1.0
        return out

    def summers(self):
        entry = np.zeros((self.groups * 128, 128), np.float32)
        leave = np.zeros((self.groups * 128, 128), np.float32)
        for g in range(self.groups):
            entry[g * 128 : (g + 1) * 128, g] = 1.0
            leave[g * 128 : (g + 1) * 128, self.groups + g] = 1.0
        return entry, leave

    def fold_rates(self, rates):
        shaped = rates.reshape(self.groups, self.fold, 1, self.halves, 128).transpose(3, 0, 1, 2, 4)
        wide = jnp.broadcast_to(shaped, (self.halves, self.groups, self.fold, self.seqs, 128))
        return wide.reshape(self.held, 8, 128)


NX = 2

PAR_SBIAS = 0
PAR_CBIAS = MODES
PAR_SKIP = MODES + 1
PAR_TAPS = MODES + 2
PAR_RATES = MODES + 2 + CONV
PAR_ROWS = 32
SUM_LOG = 8


def params_of(shape_like):
    return pltpu.CompilerParams(vmem_limit_bytes=shape_like * MIB)


def whole(shape):
    return pl.BlockSpec(shape, lambda *_: (0,) * len(shape), pipeline_mode=pl.Buffered(1))


def kept(shape):
    return pl.BlockSpec(shape, lambda *_: (0,) * len(shape))


def packed(index, seqs):
    return pl.BlockSpec((seqs, XCOLS, MBLK), index)


def packed_shape(blocks, kind=BF16):
    return jax.ShapeDtypeStruct((blocks, XCOLS, MBLK), kind)


def front_kernel(
    plan, modes, x_ref, w_ref, wx_ref, par_ref, inner_ref, gate_ref, pre_ref, act_ref, proj_ref, halo
):
    j = pl.program_id(0)
    channels = plan.chan

    @pl.when(j == 0)
    def _():
        halo[...] = jnp.zeros_like(halo)

    for q in range(plan.seqs):
        mode = modes[j * plan.seqs + q]
        joint = nn_dot(x_ref[q], w_ref[mode])
        inner_low = joint[:, :channels].astype(BF16)
        gate_ref[q] = joint[:, channels:]
        inner_ref[q] = inner_low
        inner = inner_low.astype(F32)
        wide = jnp.concatenate([halo[q], inner], 0)
        halo[q] = inner[MBLK - 8 :]
        pre = par_ref[PAR_CBIAS : PAR_CBIAS + 1, :]
        for k in range(CONV):
            pre = pre + par_ref[PAR_TAPS + k : PAR_TAPS + k + 1, :] * wide[5 + k : 5 + k + MBLK]
        pre_ref[q] = pre
        act_low = (pre * sigmoid(pre)).astype(BF16)
        act_ref[q] = act_low
        proj_ref[q, :MBLK] = nt_dot(act_low, wx_ref[mode, :RANK]).astype(BF16)
        proj_ref[q, MBLK:] = nt_dot(wx_ref[mode, RANK:], act_low).astype(BF16)


def front(plan, modes, normal, w_in, w_x, par):
    nb, seqs, chan = plan.nb, plan.seqs, plan.chan

    def rows(width):
        return pl.BlockSpec((seqs, MBLK, width), lambda j, *_: (j, 0, 0))

    def out(width, kind):
        return jax.ShapeDtypeStruct((nb * seqs, MBLK, width), kind)

    return pl.pallas_call(
        functools.partial(front_kernel, plan),
        grid_spec=pltpu.PrefetchScalarGridSpec(
            num_scalar_prefetch=1,
            grid=(nb,),
            in_specs=[rows(D), whole(w_in.shape), whole(w_x.shape), whole(par.shape)],
            out_specs=[rows(chan), rows(chan), rows(chan), rows(chan), packed(lambda j, *_: (j, 0, 0), seqs)],
            scratch_shapes=[VMEM((seqs, 8, chan), F32)],
        ),
        out_shape=[out(chan, BF16), out(chan, F32), out(chan, F32), out(chan, BF16), packed_shape(nb * seqs)],
        compiler_params=params_of(60),
        cost_estimate=pl.CostEstimate(
            flops=2 * nb * seqs * MBLK * D * 2 * chan, bytes_accessed=24 * MIB, transcendentals=0
        ),
        name="front",
    )(modes, normal, w_in, w_x, par)


def step_inputs(plan, mode, proj, wdt_ref, par_ref):
    rank_low = proj[:MBLK]
    raw = nt_dot(rank_low, wdt_ref[mode])
    biased = raw + par_ref[pl.ds(PAR_SBIAS + mode, 1), :]
    return rank_low, biased


def scan_kernel(
    plan, modes, proj_ref, act_ref, gate_ref, wdt_ref, wout_ref, par_ref, rates_ref, sel_ref,
    scanned_ref, mixed_ref, before_ref, last_ref, *refs,
):
    part_refs, (st, dr, el, yy, state) = refs[:-5], refs[-5:]
    j = pl.program_id(0)
    groups = plan.groups
    count = plan.nb * plan.seqs
    here_x, here_y = modes[count], modes[count + 1]

    @pl.when(j == 0)
    def _():
        state[...] = jnp.zeros_like(state)

    for q in range(plan.seqs):
        mode = modes[j * plan.seqs + q]
        proj = proj_ref[q]
        _, biased = step_inputs(plan, mode, proj, wdt_ref, par_ref)
        steps = softplus(biased)
        drive = steps * act_ref[q].astype(F32)
        for f in range(plan.fold):
            at = pl.ds(plan.sub(f, q), MBLK, stride=8)
            el[at, :] = tn_dot(proj[MBLK:], sel_ref[f])
            for c in range(plan.halves):
                st[c, at, :] = steps[:, c * 128 : (c + 1) * 128]
                dr[c, at, :] = drive[:, c * 128 : (c + 1) * 128]

    unroll = 16

    def some_steps(i, carry):
        now = list(carry)
        for u in range(unroll):
            t = i * unroll + u
            rows = pl.ds(pl.multiple_of(t * 8, 8), 8)
            pair = el[rows, :]
            entry = [jnp.broadcast_to(pair[:, g : g + 1], (8, 128)) for g in range(groups)]
            leave = [jnp.broadcast_to(pair[:, groups + g : groups + g + 1], (8, 128)) for g in range(groups)]
            for c in range(plan.halves):
                step = st[c, rows, :]
                drive = dr[c, rows, :]
                total = None
                for g in range(groups):
                    v = c * groups + g
                    before_ref[t, v] = now[v]
                    now[v] = jnp.exp2(step * rates_ref[v]) * now[v] + drive * entry[g]
                    term = now[v] * leave[g]
                    total = term if total is None else total + term
                yy[c, rows, :] = total
        return tuple(now)

    final = lax.fori_loop(0, MBLK // unroll, some_steps, tuple(state[v] for v in range(plan.held)))
    for v in range(plan.held):
        state[v] = final[v]
        last_ref[v] = final[v]

    skip = par_ref[PAR_SKIP : PAR_SKIP + 1, :]
    for q in range(plan.seqs):
        mode = modes[j * plan.seqs + q]
        parts = []
        for c in range(plan.halves):
            total = yy[c, pl.ds(plan.sub(0, q), MBLK, stride=8), :]
            for f in range(1, plan.fold):
                total = total + yy[c, pl.ds(plan.sub(f, q), MBLK, stride=8), :]
            parts.append(total)
        scanned = parts[0] if len(parts) == 1 else jnp.concatenate(parts, 1)
        scanned_ref[q] = scanned
        gate = gate_ref[q]
        mixed = ((scanned + skip * act_ref[q].astype(F32)) * (gate * sigmoid(gate))).astype(BF16)
        mixed_ref[q] = mixed
        dx = lax.rem(lax.rem(j, NX) + here_x, NX)
        dy = lax.rem(q + here_y, plan.seqs)
        product = nn_dot(mixed, wout_ref[mode]).astype(BF16)
        for r, part_ref in enumerate(part_refs):

            @pl.when(dx * plan.seqs + dy == r)
            def _():
                part_ref[0] = product


def forward_scan(plan, modes, proj, act, gate, w_dt, w_out, par, rates, select):
    nb, seqs, chan, held = plan.nb, plan.seqs, plan.chan, plan.held
    halves = VMEM((plan.halves, MBLK * 8, 128), F32)
    plane = NX * seqs

    def rows(width):
        return pl.BlockSpec((seqs, MBLK, width), lambda j, *_: (j, 0, 0))

    def out(width, kind):
        return jax.ShapeDtypeStruct((nb * seqs, MBLK, width), kind)

    return pl.pallas_call(
        functools.partial(scan_kernel, plan),
        grid_spec=pltpu.PrefetchScalarGridSpec(
            num_scalar_prefetch=1,
            grid=(nb,),
            in_specs=[
                packed(lambda j, *_: (j, 0, 0), seqs), rows(chan), rows(chan), whole(w_dt.shape), whole(w_out.shape),
                whole(par.shape), whole(rates.shape), whole(select.shape),
            ],
            out_specs=[
                rows(chan), rows(chan),
                pl.BlockSpec((MBLK, held, 8, 128), lambda j, *_: (j, 0, 0, 0)),
                kept((held, 8, 128)),
                *[pl.BlockSpec((1, MBLK, D), lambda j, *_: (j // NX, 0, 0))] * plane,
            ],
            scratch_shapes=[halves, halves, VMEM((MBLK * 8, 128), F32), halves, VMEM((held, 8, 128), F32)],
        ),
        out_shape=[
            out(chan, F32), out(chan, BF16),
            jax.ShapeDtypeStruct((nb * MBLK, held, 8, 128), F32),
            jax.ShapeDtypeStruct((held, 8, 128), F32),
            *[jax.ShapeDtypeStruct((nb // NX, MBLK, D), BF16)] * plane,
        ],
        compiler_params=params_of(60),
        cost_estimate=pl.CostEstimate(
            flops=60 * nb * MBLK * held * 1024, bytes_accessed=150 * MIB, transcendentals=nb * MBLK * held * 1024
        ),
        name="forward_scan",
    )(modes, proj, act, gate, w_dt, w_out, par, rates, select)


def back_kernel(
    plan, modes, cot_ref, x_ref, proj_ref, act_ref, gate_ref, scanned_ref, mixed_ref, before_ref, last_ref,
    wdt_ref, wout_ref, par_ref, rates_ref, sel_ref, sume_ref, suml_ref,
    bact_ref, bgate_ref, bproj_ref, dtg_ref, outg_ref, ing_ref, sums_ref,
    logr_ref, st, dr, el, bs, aa, uu, pe, plv, carry_ref, after_ref,
):
    i = pl.program_id(0)
    j = plan.nb - 1 - i
    groups = plan.groups

    @pl.when(i == 0)
    def _():
        carry_ref[...] = jnp.zeros_like(carry_ref)
        after_ref[...] = last_ref[...]
        dtg_ref[...] = jnp.zeros_like(dtg_ref)
        outg_ref[...] = jnp.zeros_like(outg_ref)
        ing_ref[...] = jnp.zeros_like(ing_ref)
        sums_ref[...] = jnp.zeros_like(sums_ref)
        logr_ref[...] = jnp.zeros_like(logr_ref)

    skip = par_ref[PAR_SKIP : PAR_SKIP + 1, :]
    held = []
    for q in range(plan.seqs):
        mode = modes[j * plan.seqs + q]
        proj = proj_ref[q]
        rank_low, biased = step_inputs(plan, mode, proj, wdt_ref, par_ref)
        steps = softplus(biased)
        act = act_ref[q].astype(F32)
        drive = steps * act
        back_mixed = nt_dot(cot_ref[q], wout_ref[mode])
        gate = gate_ref[q]
        sig = sigmoid(gate)
        back_scanned = back_mixed * (gate * sig)
        slope = sig * (1.0 + gate * (1.0 - sig))
        back_gate = (back_mixed * (scanned_ref[q] + skip * act) * slope).astype(BF16)
        bgate_ref[q] = back_gate
        add_outer(ing_ref, mode, x_ref, q, back_gate)
        outg_ref[mode] += tn_dot(mixed_ref[q], cot_ref[q])
        for f in range(plan.fold):
            at = pl.ds(plan.sub(f, q), MBLK, stride=8)
            el[at, :] = tn_dot(proj[MBLK:], sel_ref[f])
            for c in range(plan.halves):
                cols = slice(c * 128, (c + 1) * 128)
                st[c, at, :] = steps[:, cols]
                dr[c, at, :] = drive[:, cols]
                bs[c, at, :] = back_scanned[:, cols]
        held.append((mode, rank_low, biased, steps, act, back_scanned))

    unroll = 16

    def some_steps(i, carry):
        lam_in = list(carry[0])
        after = list(carry[1])
        log_sum = list(carry[2])
        for u in range(unroll):
            t = MBLK - 1 - (i * unroll + u)
            rows = pl.ds(pl.multiple_of(t * 8, 8), 8)
            pair = el[rows, :]
            entry = [jnp.broadcast_to(pair[:, g : g + 1], (8, 128)) for g in range(groups)]
            leave = [jnp.broadcast_to(pair[:, groups + g : groups + g + 1], (8, 128)) for g in range(groups)]
            entry_sum, leave_sum = [None] * groups, [None] * groups
            for c in range(plan.halves):
                step = st[c, rows, :]
                drive = dr[c, rows, :]
                push = bs[c, rows, :]
                a_sum = None
                u_sum = None
                for g in range(groups):
                    v = c * groups + g
                    rate = rates_ref[v]
                    before = before_ref[t, v]
                    lam = push * leave[g] + lam_in[v]
                    leave_term = push * after[v]
                    entry_term = lam * drive
                    leave_sum[g] = leave_term if c == 0 else leave_sum[g] + leave_term
                    entry_sum[g] = entry_term if c == 0 else entry_sum[g] + entry_term
                    moved = lam * jnp.exp2(step * rate)
                    lam_in[v] = moved
                    after[v] = before
                    felt = moved * before
                    a_term = rate * felt
                    u_term = lam * entry[g]
                    a_sum = a_term if a_sum is None else a_sum + a_term
                    u_sum = u_term if u_sum is None else u_sum + u_term
                    log_sum[v] = log_sum[v] + step * felt
                aa[c, rows, :] = a_sum
                uu[c, rows, :] = u_sum
            for g in range(groups):
                cols = slice(g * 128, (g + 1) * 128)
                pe[rows, cols] = entry_sum[g]
                plv[rows, cols] = leave_sum[g]
        return (tuple(lam_in), tuple(after), tuple(log_sum))

    start = (
        tuple(carry_ref[v] for v in range(plan.held)),
        tuple(after_ref[v] for v in range(plan.held)),
        tuple(logr_ref[v] for v in range(plan.held)),
    )
    lam_end, after_end, log_end = lax.fori_loop(0, MBLK // unroll, some_steps, start)
    for v in range(plan.held):
        carry_ref[v] = lam_end[v]
        after_ref[v] = after_end[v]
        logr_ref[v] = log_end[v]

    el[...] = nn_dot(pe[...].astype(BF16), sume_ref[...]) + nn_dot(plv[...].astype(BF16), suml_ref[...])

    for q in range(plan.seqs):
        mode, rank_low, biased, steps, act, back_scanned = held[q]
        a_parts, u_parts = [], []
        back_pair = jnp.zeros((2 * STATE, MBLK), F32)
        for c in range(plan.halves):
            a_total, u_total = None, None
            for f in range(plan.fold):
                at = pl.ds(plan.sub(f, q), MBLK, stride=8)
                a_term, u_term = aa[c, at, :], uu[c, at, :]
                a_total = a_term if a_total is None else a_total + a_term
                u_total = u_term if u_total is None else u_total + u_term
            a_parts.append(a_total * LN2)
            u_parts.append(u_total)
        for f in range(plan.fold):
            both = el[pl.ds(plan.sub(f, q), MBLK, stride=8), :]
            back_pair = back_pair + nt_dot(sel_ref[f], both.astype(BF16))
        a_all = a_parts[0] if len(a_parts) == 1 else jnp.concatenate(a_parts, 1)
        u_all = u_parts[0] if len(u_parts) == 1 else jnp.concatenate(u_parts, 1)
        back_steps = a_all + act * u_all
        bact_ref[q] = skip * back_scanned + steps * u_all
        back_pre_step = back_steps * sigmoid(biased)
        raw_low = back_pre_step.astype(BF16)
        bproj_ref[q, :MBLK] = nn_dot(raw_low, wdt_ref[mode]).astype(BF16)
        bproj_ref[q, MBLK:] = back_pair.astype(BF16)
        dtg_ref[mode] += tn_dot(raw_low, rank_low)
        sums_ref[pl.ds(mode, 1), :] += jnp.sum(back_pre_step, 0, keepdims=True)
        sums_ref[MODES : MODES + 1, :] += jnp.sum(back_scanned * act, 0, keepdims=True)

    @pl.when(j == 0)
    def _():
        for v in range(plan.held):
            c, g = v // groups, v % groups
            for f in range(plan.fold):
                at = plan.sub(f, 0)
                total = jnp.sum(logr_ref[v, at : at + plan.seqs, :], 0, keepdims=True)
                n = SUM_LOG + g * plan.fold + f
                scaled = total * rates_ref[v, at : at + 1, :] * LN2
                sums_ref[n : n + 1, c * 128 : (c + 1) * 128] = scaled


def backward_scan(plan, modes, cot, normal, proj, act, gate, scanned, mixed, before, last, w_dt, w_out, par, rates, select):
    nb, seqs, chan, groups, held = plan.nb, plan.seqs, plan.chan, plan.groups, plan.held
    sum_entry, sum_leave = plan.summers()
    sum_entry, sum_leave = jnp.asarray(sum_entry, BF16), jnp.asarray(sum_leave, BF16)

    def rows(width):
        return pl.BlockSpec((seqs, MBLK, width), lambda i, *_: (nb - 1 - i, 0, 0))

    def out(width, kind):
        return jax.ShapeDtypeStruct((nb * seqs, MBLK, width), kind)

    tall = VMEM((plan.halves, MBLK * 8, 128), F32)
    return pl.pallas_call(
        functools.partial(back_kernel, plan),
        grid_spec=pltpu.PrefetchScalarGridSpec(
            num_scalar_prefetch=1,
            grid=(nb,),
            in_specs=[
                rows(D), rows(D), packed(lambda i, *_: (nb - 1 - i, 0, 0), seqs),
                rows(chan), rows(chan), rows(chan), rows(chan),
                pl.BlockSpec((MBLK, held, 8, 128), lambda i, *_: (nb - 1 - i, 0, 0, 0)),
                whole(last.shape), whole(w_dt.shape), whole(w_out.shape), whole(par.shape),
                whole(rates.shape), whole(select.shape),
                whole(sum_entry.shape), whole(sum_leave.shape),
            ],
            out_specs=[
                rows(chan), rows(chan), packed(lambda i, *_: (nb - 1 - i, 0, 0), seqs),
                kept((MODES, chan, RANK)), kept((MODES, chan, D)), kept((MODES, D, chan)),
                kept((SUM_LOG + STATE, chan)),
            ],
            scratch_shapes=[
                VMEM((held, 8, 128), F32), tall, tall, VMEM((MBLK * 8, 128), F32), tall, tall, tall,
                VMEM((MBLK * 8, groups * 128), F32), VMEM((MBLK * 8, groups * 128), F32),
                VMEM((held, 8, 128), F32), VMEM((held, 8, 128), F32),
            ],
        ),
        out_shape=[
            out(chan, F32), out(chan, BF16), packed_shape(nb * seqs),
            jax.ShapeDtypeStruct((MODES, chan, RANK), F32),
            jax.ShapeDtypeStruct((MODES, chan, D), F32),
            jax.ShapeDtypeStruct((MODES, D, chan), F32),
            jax.ShapeDtypeStruct((SUM_LOG + STATE, chan), F32),
        ],
        compiler_params=params_of(60),
        cost_estimate=pl.CostEstimate(
            flops=100 * nb * MBLK * held * 1024, bytes_accessed=300 * MIB, transcendentals=nb * MBLK * held * 1024
        ),
        name="backward_scan",
    )(modes, cot, normal, proj, act, gate, scanned, mixed, before, last, w_dt, w_out, par, rates, select,
      sum_entry, sum_leave)


def tail_kernel(
    plan, modes, bp_ref, bact_ref, bgate_ref, pre_ref, act_ref, inner_ref, earlier_ref, x_ref,
    wx_ref, par_ref,
    joint_ref, ing_ref, xg_ref, sums_ref,
    halo,
):
    i = pl.program_id(0)
    j = plan.nb - 1 - i
    channels = plan.chan

    @pl.when(i == 0)
    def _():
        halo[...] = jnp.zeros_like(halo)
        ing_ref[...] = jnp.zeros_like(ing_ref)
        xg_ref[...] = jnp.zeros_like(xg_ref)
        sums_ref[...] = jnp.zeros_like(sums_ref)

    first = jnp.where(j == 0, 0.0, 1.0)
    for q in range(plan.seqs):
        mode = modes[j * plan.seqs + q]
        rank_low, pair_low = bp_ref[q, :MBLK], bp_ref[q, MBLK:]
        back_act = bact_ref[q] + nn_dot(rank_low, wx_ref[mode, :RANK]) + tn_dot(pair_low, wx_ref[mode, RANK:])
        xg_ref[mode, :RANK] += tn_dot(rank_low, act_ref[q])
        xg_ref[mode, RANK:] += nn_dot(pair_low, act_ref[q])
        pre = pre_ref[q]
        sig = sigmoid(pre)
        back_pre = back_act * (sig * (1.0 + pre * (1.0 - sig)))
        wide = jnp.concatenate([back_pre, halo[q]], 0)
        halo[q] = back_pre[:8]
        inner_wide = jnp.concatenate(
            [earlier_ref[q][MBLK - 16 :].astype(F32) * first, inner_ref[q].astype(F32)], 0
        )
        back_inner = None
        for k in range(CONV):
            term = par_ref[PAR_TAPS + k : PAR_TAPS + k + 1, :] * wide[CONV - 1 - k : CONV - 1 - k + MBLK]
            back_inner = term if back_inner is None else back_inner + term
            felt = back_pre * inner_wide[13 + k : 13 + k + MBLK]
            sums_ref[k : k + 1, :] += jnp.sum(felt, 0, keepdims=True)
        sums_ref[CONV : CONV + 1, :] += jnp.sum(back_pre, 0, keepdims=True)
        inner_low = back_inner.astype(BF16)
        joint_low = jnp.concatenate([inner_low, bgate_ref[q]], 1)
        joint_ref[q] = joint_low
        add_outer(ing_ref, mode, x_ref, q, inner_low)


def tail(plan, modes, bp, bact, bgate, pre, act, inner, normal, w_x, par):
    nb, seqs, chan = plan.nb, plan.seqs, plan.chan

    def rows(width):
        return pl.BlockSpec((seqs, MBLK, width), lambda i, *_: (nb - 1 - i, 0, 0))

    return pl.pallas_call(
        functools.partial(tail_kernel, plan),
        grid_spec=pltpu.PrefetchScalarGridSpec(
            num_scalar_prefetch=1,
            grid=(nb,),
            in_specs=[
                packed(lambda i, *_: (nb - 1 - i, 0, 0), seqs), rows(chan), rows(chan), rows(chan), rows(chan), rows(chan),
                pl.BlockSpec((seqs, MBLK, chan), lambda i, *_: (jnp.maximum(nb - 2 - i, 0), 0, 0)),
                rows(D), whole(w_x.shape), whole(par.shape),
            ],
            out_specs=[
                rows(2 * chan), kept((MODES, D, chan)), kept((MODES, XCOLS, chan)),
                kept((8, chan)),
            ],
            scratch_shapes=[VMEM((seqs, 8, chan), F32)],
        ),
        out_shape=[
            jax.ShapeDtypeStruct((nb * seqs, MBLK, 2 * chan), BF16),
            jax.ShapeDtypeStruct((MODES, D, chan), F32),
            jax.ShapeDtypeStruct((MODES, XCOLS, chan), F32),
            jax.ShapeDtypeStruct((8, chan), F32),
        ],
        compiler_params=params_of(60),
        cost_estimate=pl.CostEstimate(
            flops=4 * nb * seqs * MBLK * D * 2 * chan, bytes_accessed=40 * MIB, transcendentals=0
        ),
        name="tail",
    )(modes, bp, bact, bgate, pre, act, inner, inner, normal, w_x, par)


ANY = pl.ANY
DMA = pltpu.SemaphoreType.DMA


def any_spec():
    return pl.BlockSpec(memory_space=ANY)


def vmem_spec():
    return pl.BlockSpec(memory_space=VMEM)


def remote(src, dst, send, recv, device):
    return pltpu.make_async_remote_copy(
        src_ref=src, dst_ref=dst, send_sem=send, recv_sem=recv, device_id=device,
        device_id_type=pl.DeviceIdType.MESH,
    )


class Place:
    def __init__(self, dims):
        self.ns, self.ny, self.nl = dims
        self.nz = self.ns // NX
        self.groups = self.ns * self.ny
        self.devices = self.groups * self.nl
        seq = lax.axis_index("seq")
        self.z, self.x = lax.div(seq, NX), lax.rem(seq, NX)
        self.y = lax.axis_index("hi")
        self.l = lax.axis_index("lo")
        self.g = seq * self.ny + self.y
        self.i = self.g * self.nl + self.l
        self.ox, self.oy = NX - 1 - self.x, self.ny - 1 - self.y

    def device(self, z, x, y, low):
        return (z * NX + x, y, low)

    def of_group(self, g, low):
        return (lax.div(g, self.ny), lax.rem(g, self.ny), low)

    def of_index(self, i):
        return self.of_group(lax.div(i, self.nl), lax.rem(i, self.nl))

    def group(self, z, x, y):
        return (z * NX + x) * self.ny + y

    def relative(self, n, sign):
        plane = NX * self.ny
        dz, rest = lax.div(n, plane), lax.rem(n, plane)
        dx, dy = lax.div(rest, self.ny), lax.rem(rest, self.ny)
        z = lax.rem(self.z + self.nz + sign * dz, self.nz)
        x = lax.rem(self.x + NX + sign * dx, NX)
        y = lax.rem(self.y + self.ny + sign * dy, self.ny)
        return self.group(z, x, y)

    def in_plane(self, z, r):
        x = lax.rem(self.x + lax.div(r, self.ny), NX)
        y = lax.rem(self.y + lax.rem(r, self.ny), self.ny)
        return self.group(z, x, y)

    def after(self, n):
        return self.relative(jnp.int32(n), 1)

    def before(self, n):
        return self.relative(jnp.int32(n), -1)

    def x_peer(self):
        return self.device(self.z, self.ox, self.y, self.l)

    def y_peer(self):
        return self.device(self.z, self.x, self.oy, self.l)

    def z_after(self, k):
        return lax.rem(self.z + k, self.nz)

    def z_before(self, k):
        return lax.rem(self.z + self.nz - k, self.nz)

    def z_peer(self, k):
        return self.device(self.z_after(k), self.x, self.y, self.l)

    def low_after(self, k):
        return lax.rem(self.l + k, self.nl)

    def low_before(self, k):
        return lax.rem(self.l + self.nl - k, self.nl)

    def low_peer(self, k):
        return self.device(self.z, self.x, self.y, self.low_after(k))


def lanes_shape(rows, parts, width):
    return (rows, parts * width) if width % 128 == 0 else (parts, rows, width)


def lanes_at(ref, part, width):
    if width % 128 == 0:
        return ref.at[:, pl.ds(pl.multiple_of(part * width, width), width)]
    return ref.at[part]


def lanes_join(array):
    return array if array.ndim == 2 else jnp.swapaxes(array, 0, 1).reshape(array.shape[1], -1)


def lanes_split(array, parts):
    width = array.shape[1] // parts
    return array if width % 128 == 0 else array.reshape(array.shape[0], parts, width).swapaxes(0, 1)


def greet_all(here):
    barrier = pltpu.get_barrier_semaphore()

    def greet(k, carry):
        peer = here.of_index(lax.rem(here.i + k, here.devices))
        pl.semaphore_signal(barrier, inc=1, device_id=peer, device_id_type=pl.DeviceIdType.MESH)
        return carry

    lax.fori_loop(1, here.devices, greet, 0)
    pl.semaphore_wait(barrier, here.devices - 1)


def greet_near(here, low_too):
    barrier = pltpu.get_barrier_semaphore()
    peers = [here.x_peer()]
    if here.ny > 1:
        peers.append(here.y_peer())
    peers += [here.z_peer(k) for k in range(1, here.nz)]
    if low_too:
        peers += [here.low_peer(k) for k in range(1, here.nl)]
    for peer in peers:
        pl.semaphore_signal(barrier, inc=1, device_id=peer, device_id_type=pl.DeviceIdType.MESH)
    pl.semaphore_wait(barrier, len(peers))


def gather_sems(dims):
    nz = dims[0] // NX
    return [DMA((1,))] + [DMA((nz, 2))] * 6


def in_line(dims):
    return dims[0] // NX <= 4


class Gather:
    def __init__(self, here, own, out, rows, sems, line):
        self.here, self.own, self.out, self.half, self.line = here, own, out, rows // 2, line
        self.local, self.up, self.down, self.xs, self.ys, self.fx, self.fy = sems

    def block(self, z, x, y):
        return self.out.at[self.here.group(z, x, y)]

    def mine(self, z):
        return self.block(z, self.here.x, self.here.y)

    def keep(self):
        return pltpu.make_async_copy(self.own, self.out.at[self.here.g], self.local.at[0])

    def next(self, src, dst, sems, d, step):
        here = self.here
        peer = here.device(here.z + step, here.x, here.y, here.l)
        return remote(src, dst, sems.at[d, 0], sems.at[d, 1], peer)

    def far(self, k):
        here = self.here
        return remote(self.own, self.out.at[here.g], self.up.at[k, 0], self.up.at[k, 1], here.z_peer(k))

    def cross(self, z, src):
        here = self.here
        dst = self.mine(z)
        out = [remote(src, dst, self.xs.at[z, 0], self.xs.at[z, 1], here.x_peer())]
        if here.ny > 1:
            out.append(remote(src, dst, self.ys.at[z, 0], self.ys.at[z, 1], here.y_peer()))
        return out

    def spread(self, z, src):
        for copy in self.cross(z, src):
            copy.start()

    def start(self):
        here = self.here
        self.keep().start()
        if self.line:
            at = self.out.at[here.g]

            @pl.when(here.z + 1 < here.nz)
            def _():
                self.next(self.own, at, self.up, 0, 1).start()

            @pl.when(here.z > 0)
            def _():
                self.next(self.own, at, self.down, 0, -1).start()

        else:
            for k in range(1, here.nz):
                self.far(k).start()
        self.spread(here.z, self.own)

    def step(self, d):
        here = self.here
        if not self.line:
            z = here.z_before(d)
            self.far(d).wait_recv()
            self.spread(z, self.mine(z))
            return
        for sems, sign in ((self.up, 1), (self.down, -1)):
            z = here.z - sign * d
            on = here.z + sign

            @pl.when((z >= 0) & (z < here.nz))
            def _():
                got = self.mine(z)
                self.next(got, got, sems, d - 1, -sign).wait_recv()

                @pl.when((on >= 0) & (on < here.nz))
                def _():
                    self.next(got, got, sems, d, sign).start()

                self.spread(z, got)

    def halves(self, z, first):
        here = self.here
        to_y = self.block(z, here.ox, here.y) if first else self.block(z, here.ox, here.oy)
        to_x = self.block(z, here.x, here.oy) if first else self.block(z, here.ox, here.oy)
        upper, lower = to_y.at[pl.ds(0, self.half)], to_x.at[pl.ds(self.half, self.half)]
        return (
            remote(upper, upper, self.fy.at[z, 0], self.fy.at[z, 1], here.y_peer()),
            remote(lower, lower, self.fx.at[z, 0], self.fx.at[z, 1], here.x_peer()),
        )

    def forward(self, z):
        here = self.here
        copies = self.cross(z, self.mine(z))
        copies[0].wait_recv()
        if here.ny > 1:
            to_y, to_x = self.halves(z, True)
            to_y.start()
            copies[1].wait_recv()
            to_x.start()

    def forward_all(self):
        here = self.here
        self.forward(here.z)
        for d in range(1, here.nz):
            if self.line:
                for z in (here.z - d, here.z + d):

                    @pl.when((z >= 0) & (z < here.nz))
                    def _():
                        self.forward(z)

            else:
                self.forward(here.z_before(d))

    def end(self):
        here = self.here
        self.keep().wait()

        def finish(z, carry):
            for copy in self.cross(z, self.mine(z)):
                copy.wait_send()
            if here.ny > 1:
                for copy in self.halves(z, False):
                    copy.wait()
            return carry

        lax.fori_loop(0, here.nz, finish, 0)
        if not self.line:
            for k in range(1, here.nz):
                self.far(k).wait_send()
            return
        for sems, sign in ((self.up, 1), (self.down, -1)):
            on = here.z + sign
            for d in range(here.nz):
                z = here.z - sign * d

                @pl.when((z >= 0) & (z < here.nz) & (on >= 0) & (on < here.nz))
                def _():
                    self.next(self.mine(z), self.mine(z), sems, d, sign).wait_send()


def reduce_scratch(dims, rows, width, kind):
    ns, ny, _ = dims
    nz = ns // NX
    ra = rows // 2 if ny > 1 else rows
    rb = rows // 2
    out = [
        VMEM((nz, ny, ra, width), kind), VMEM((rows, width), F32),
        VMEM((nz, rows, width), kind), VMEM((nz, rows, width), kind),
        VMEM((1, 16, 128), kind),
        DMA((nz, 2)), DMA((nz, 2)), DMA((nz, 2)), DMA((nz, 2)), DMA((nz, 2)), DMA((nz, 2)),
    ]
    if ny > 1:
        out += [VMEM((nz, NX, rb, width), kind)] + [VMEM((nz, rb, width), kind)] * 4
    return out


class Reduce:
    def __init__(self, here, part, rows, bufs, line):
        self.here, self.part, self.line = here, part, line
        self.r1a, self.acc, self.s3, self.r3, self.r3d = bufs[:5]
        self.s1, self.s1b, self.s2, self.s2b, self.up, self.down = bufs[5:11]
        self.two = here.ny > 1
        ra = rows // 2 if self.two else rows
        self.top, self.low = pl.ds(0, ra), pl.ds(ra, rows - ra)
        if self.two:
            self.r1b, self.t2a, self.r2a, self.t2b, self.r2b = bufs[11:]

    def target(self, k):
        if not self.line:
            return self.here.z_after(k + 1)
        k = jnp.int32(k)
        half = lax.div(k, 2)
        return jnp.where(lax.rem(k, 2) == 0, self.here.nz - 1 - half, half)

    def copies(self, k):
        here, part, z = self.here, self.part, self.target(k)
        out = [remote(part.at[z, here.ox, :, self.top], self.r1a.at[k], self.s1.at[k, 0], self.s1.at[k, 1], here.x_peer())]
        if self.two:
            out.append(
                remote(part.at[z, :, here.oy, self.low], self.r1b.at[k], self.s1b.at[k, 0], self.s1b.at[k, 1], here.y_peer())
            )
        return out

    def crossed(self, k):
        here = self.here
        return (
            remote(self.t2a.at[k], self.r2a.at[k], self.s2.at[k, 0], self.s2.at[k, 1], here.y_peer()),
            remote(self.t2b.at[k], self.r2b.at[k], self.s2b.at[k, 0], self.s2b.at[k, 1], here.x_peer()),
        )

    def first(self, k):
        for copy in self.copies(k):
            copy.start()

    def second(self, k):
        here, part, z = self.here, self.part, self.target(k)
        kind = part.dtype
        copies = self.copies(k)
        copies[0].wait_recv()
        if self.two:
            total = part[z, here.x, here.oy, self.top].astype(F32) + self.r1a[k, here.oy].astype(F32)
            self.t2a[k] = total.astype(kind)
            a, b = self.crossed(k)
            a.start()
            copies[1].wait_recv()
            total = part[z, here.ox, here.y, self.low].astype(F32) + self.r1b[k, here.ox].astype(F32)
            self.t2b[k] = total.astype(kind)
            b.start()

    def totals(self, k):
        here, part, z = self.here, self.part, self.target(k)
        out = [(self.top, part[z, here.x, here.y, self.top].astype(F32) + self.r1a[k, here.y].astype(F32))]
        if self.two:
            for copy in self.crossed(k):
                copy.wait_recv()
            lower = part[z, here.x, here.y, self.low].astype(F32) + self.r1b[k, here.x].astype(F32)
            out = [(self.top, out[0][1] + self.r2a[k].astype(F32)), (self.low, lower + self.r2b[k].astype(F32))]
        return out

    def flows(self):
        return ((self.up, self.r3, 1), (self.down, self.r3d, -1))

    def along(self, z, sems, slot, step):
        here = self.here
        peer = here.device(here.z + step, here.x, here.y, here.l)
        return remote(self.s3.at[z], slot.at[z], sems.at[z, 0], sems.at[z, 1], peer)

    def straight(self, k):
        return remote(self.s3.at[k], self.r3.at[k], self.up.at[k, 0], self.up.at[k, 1], self.here.z_peer(k + 1))

    def third(self, k):
        here = self.here
        kind = self.part.dtype
        z = self.target(k)
        if not self.line:
            for rows, total in self.totals(k):
                self.s3[k, rows] = total.astype(kind)
            self.straight(k).start()
            return

        @pl.when(z == here.z)
        def _():
            for rows, total in self.totals(k):
                self.acc[rows] = total

        for sems, slot, sign in self.flows():
            back = here.z - sign

            @pl.when(sign * (z - here.z) > 0)
            def _():
                totals = self.totals(k)

                @pl.when((back >= 0) & (back < here.nz))
                def _():
                    self.along(z, sems, slot, -sign).wait_recv()
                    for rows, total in totals:
                        self.s3[z, rows] = (total + slot[z, rows].astype(F32)).astype(kind)

                @pl.when((back < 0) | (back >= here.nz))
                def _():
                    for rows, total in totals:
                        self.s3[z, rows] = total.astype(kind)

                self.along(z, sems, slot, sign).start()

    def last(self):
        here = self.here
        if not self.line:
            for rows, total in self.totals(here.nz - 1):
                self.acc[rows] = total

            def add(k, carry):
                self.straight(k).wait_recv()
                self.acc[...] += self.r3[k].astype(F32)
                return carry

            lax.fori_loop(0, here.nz - 1, add, 0)
            return
        for sems, slot, sign in self.flows():
            back = here.z - sign

            @pl.when((back >= 0) & (back < here.nz))
            def _():
                self.along(here.z, sems, slot, -sign).wait_recv()
                self.acc[...] += slot[here.z].astype(F32)

    def end(self):
        here = self.here

        def finish(k, carry):
            for copy in self.copies(k):
                copy.wait_send()
            if self.two:
                for copy in self.crossed(k):
                    copy.wait_send()
            return carry

        lax.fori_loop(0, here.nz, finish, 0)
        if not self.line:
            for k in range(here.nz - 1):
                self.straight(k).wait_send()
            return
        for z in range(here.nz):
            for sems, slot, sign in self.flows():

                @pl.when(sign * (z - here.z) > 0)
                def _():
                    self.along(z, sems, slot, sign).wait_send()


def comm_params(name_id, mib):
    return pltpu.CompilerParams(collective_id=name_id, has_side_effects=True, vmem_limit_bytes=mib * MIB)


def comm_cost(us):
    return pl.CostEstimate(flops=0, bytes_accessed=us * 3_000_000, transcendentals=0)


def entry_kernel(
    dims, small_ref, pick_ref, x_ref, win_ref, wdt_ref, wout_ref, wx_ref, chan_ref,
    modes_out, gain_out, normal_out, win_out, wdt_out, wout_out, wx_out, chan_out,
    slots, own, smalls, cols, keep, lows, weights, *gathers,
):
    here = Place(dims)
    rows_d = win_ref.shape[1]
    rows_e = wdt_ref.shape[1]
    chan = win_out.shape[2] // 2
    greet_all(here)

    def small_copy(k):
        peer = here.of_index(lax.rem(here.i + k, here.devices))
        return remote(small_ref, slots.at[here.i], smalls.at[k, 0], smalls.at[k, 1], peer)

    def send_small(k, carry):
        small_copy(k).start()
        return carry

    lax.fori_loop(1, here.devices, send_small, 0)
    slots[here.i] = small_ref[...]

    def rows_of(g, low):
        return win_out.at[:, pl.ds(pl.multiple_of((g * here.nl + low) * rows_d, rows_d), rows_d), :]

    def cols_of(g):
        dst = rows_of(here.g, here.l)
        out = []
        for side in range(2):
            at = pl.ds(pl.multiple_of(side * INNER + g * chan, chan), chan)
            out.append((win_ref.at[:, :, at], dst.at[:, :, pl.ds(side * chan, chan)]))
        return out

    def send_cols(z, r):
        g = here.in_plane(z, r)
        for side, (src, dst) in enumerate(cols_of(g)):
            to = cols.at[side, z * plane + r, 0]
            there = cols.at[side, here.z * plane + r, 1]
            remote(src, dst, to, there, here.of_group(g, here.l)).start()

    plane = NX * here.ny

    def own_copies():
        out = [
            pltpu.make_async_copy(src, dst, keep.at[5 * side]) for side, (src, dst) in enumerate(cols_of(here.g))
        ]
        for n, (src, dst) in enumerate(shared(here.l)):
            out.append(pltpu.make_async_copy(src, dst, keep.at[n + 1]))
        return out

    def shared(low):
        rows = pl.ds(pl.multiple_of(low * rows_e, rows_e), rows_e)
        return (
            (wdt_ref, wdt_out.at[:, rows, :]),
            (wout_ref, wout_out.at[:, rows, :]),
            (wx_ref, lanes_at(wx_out, low, rows_e)),
            (chan_ref, lanes_at(chan_out, low, rows_e)),
        )

    def low_copies(k):
        peer = here.low_peer(k)
        return [
            remote(src, dst, weights.at[k, n, 0], weights.at[k, n, 1], peer)
            for n, (src, dst) in enumerate(shared(here.l))
        ]

    def own_forward(k):
        return [
            remote(src, dst, lows.at[k, here.g + side * here.groups, 0], lows.at[k, here.g + side * here.groups, 1], here.low_peer(k))
            for side, (src, dst) in enumerate(cols_of(here.g))
        ]

    def col_forward(k, n, src_group, src):
        return remote(src, rows_of(src_group, here.l), lows.at[k, n, 0], lows.at[k, n, 1], here.low_peer(k))

    for copy in own_copies():
        copy.start()
    for k in range(1, here.nl):
        for copy in low_copies(k) + own_forward(k):
            copy.start()

    def wait_small(k, carry):
        small_copy(k).wait_recv()
        return carry

    lax.fori_loop(1, here.devices, wait_small, 0)
    lane = lax.broadcasted_iota(jnp.int32, (1, 128), 1)
    row = jnp.zeros((1, 128), F32)
    for g in range(here.groups):
        row = jnp.where(lane == g, slots[g * here.nl + here.l, MODES : MODES + 1, :], row)
    modes_out[...] = jnp.broadcast_to(row, (8, 128))
    x = x_ref[...].astype(F32)
    scale = lax.rsqrt(jnp.mean(x * x, -1, keepdims=True) + NORM_EPS)
    per = 128 // rows_d
    for t in range(D // 128):
        tile = slots[t * per]
        for n in range(1, per):
            tile = tile + slots[t * per + n]
        row = jnp.sum(tile * pick_ref[...], 0, keepdims=True)
        at = slice(t * 128, (t + 1) * 128)
        gain_out[:, at] = jnp.broadcast_to(row, (8, 128))
        own[:, at] = (x[:, at] * scale * row).astype(BF16)

    gather = Gather(here, own, normal_out, MBLK, gathers, in_line(dims))
    gather.start()

    def send_plane(d):
        def one(r, carry):
            z = jnp.where(lax.rem(r, 2) == 0, here.z_after(d), here.z_before(d))

            @pl.when((z != here.z) | (r > 0))
            def _():
                send_cols(z, r)

            return carry

        lax.fori_loop(0, plane, one, 0)

    send_plane(0)
    for d in range(1, here.nz):
        gather.step(d)
        send_plane(d)
    gather.forward_all()

    def each_source(act):
        def one(n, carry):
            z, r = lax.div(n, plane), lax.rem(n, plane)

            @pl.when((z != here.z) | (r > 0))
            def _():
                act(n, here.in_plane(z, r))

            return carry

        lax.fori_loop(0, here.groups, one, 0)

    def pass_cols(n, g):
        got = rows_of(g, here.l)
        for side in range(2):
            half = got.at[:, :, pl.ds(side * chan, chan)]
            remote(half, half, cols.at[side, n, 0], cols.at[side, n, 1], here.of_group(g, here.l)).wait_recv()
        for k in range(1, here.nl):
            col_forward(k, g, g, got).start()

    each_source(pass_cols)
    gather.end()

    def end_lows(n, g):
        for k in range(1, here.nl):
            mine, theirs = rows_of(g, here.l), rows_of(g, here.low_before(k))
            remote(mine, mine, lows.at[k, g, 0], lows.at[k, g, 1], here.low_peer(k)).wait_send()
            remote(theirs, theirs, lows.at[k, g, 0], lows.at[k, g, 1], here.low_peer(k)).wait_recv()

    def end_sent(n, g):
        for side in range(2):
            half = rows_of(g, here.l).at[:, :, pl.ds(side * chan, chan)]
            remote(half, half, cols.at[side, n, 0], cols.at[side, n, 1], here.x_peer()).wait_send()

    for k in range(1, here.nl):
        for copy in own_forward(k):
            copy.wait()

    def end_small(k, carry):
        small_copy(k).wait_send()
        return carry

    each_source(end_lows)
    each_source(end_sent)
    lax.fori_loop(1, here.devices, end_small, 0)
    for copy in own_copies():
        copy.wait()
    for k in range(1, here.nl):
        for n, (_, got) in enumerate(shared(here.low_before(k))):
            remote(got, got, weights.at[k, n, 0], weights.at[k, n, 1], here.low_peer(k)).wait()


def entry(dims, small, pick, x, win, wdt, wout, wx, chan):
    ns, ny, nl = dims
    groups, devices = ns * ny, ns * ny * nl
    shape = jax.ShapeDtypeStruct

    def tall(ref):
        return shape((MODES, ref.shape[1] * nl, ref.shape[2]), BF16)

    return pl.pallas_call(
        functools.partial(entry_kernel, dims),
        in_specs=[vmem_spec()] * 3 + [any_spec()] * 5,
        out_specs=[vmem_spec()] * 2 + [any_spec()] * 6,
        out_shape=[
            shape((8, 128), F32), shape((8, D), F32), shape((groups, MBLK, D), BF16),
            shape((MODES, D, win.shape[2] // groups), BF16), tall(wdt), tall(wout),
            *[shape(lanes_shape(a.shape[0], nl, a.shape[1]), a.dtype) for a in (wx, chan)],
        ],
        scratch_shapes=[
            VMEM((devices, 8, 128), F32), VMEM((MBLK, D), BF16), DMA((devices, 2)), DMA((2, groups, 2)),
            DMA((6,)), DMA((nl, 2 * groups, 2)), DMA((nl, 4, 2)), *gather_sems(dims),
        ],
        compiler_params=comm_params(1, 60),
        cost_estimate=comm_cost(100),
        name="entry",
    )(small, pick, x, win, wdt, wout, wx, chan)


def column_scratch(dims, rows_d, chan):
    ns, ny, nl = dims
    piece = (ns * ny, MODES, rows_d, chan)
    return [VMEM(piece, F32), VMEM((nl - 1,) + piece, F32), DMA((ns * ny,)), DMA((nl, ns * ny, 2))]


class Columns:
    def __init__(self, here, src, bufs):
        self.here, self.src = here, src
        self.mine, self.theirs, self.keep, self.swap = bufs

    def own_copy(self, n):
        here = self.here
        return pltpu.make_async_copy(self.src.at[:, here.after(n), here.l], self.mine.at[n], self.keep.at[n])

    def swap_copy(self, k, n):
        here = self.here
        part = self.src.at[:, here.after(n), here.low_after(k)]
        sems = self.swap.at[k, n]
        return remote(part, self.theirs.at[k - 1, n], sems.at[0], sems.at[1], here.low_peer(k))

    def begin(self):
        def one(n, carry):
            self.own_copy(n).start()
            for k in range(1, self.here.nl):
                self.swap_copy(k, n).start()
            return carry

        lax.fori_loop(0, self.here.groups, one, 0)

    def merged(self, n):
        self.own_copy(n).wait()
        total = self.mine[n]
        for k in range(1, self.here.nl):
            self.swap_copy(k, n).wait_recv()
            total = total + self.theirs[k - 1, n]
        return total.astype(BF16)

    def end(self):
        def one(n, carry):
            for k in range(1, self.here.nl):
                self.swap_copy(k, n).wait_send()
            return carry

        lax.fori_loop(0, self.here.groups, one, 0)


def share_kernel(dims, extras, part_ref, *refs):
    here = Place(dims)
    nz, plane = here.nz, NX * here.ny
    more = len(column_scratch(dims, 16, 128)) if extras else 0
    extra_in, refs = refs[:extras], refs[extras:]
    out_ref, extra_out, refs = refs[0], refs[1 : extras + 1], refs[extras + 1 :]
    near, sent, far, res, near_sems, far_sems, back_sems, wide_sems, keep, pairs = refs[:10]
    columns = refs[10 : 10 + more]
    spot = here.x * here.ny + here.y

    def partner(r):
        x = lax.rem(here.x + r // here.ny, NX)
        y = lax.rem(here.y + r % here.ny, here.ny)
        return x * here.ny + y, here.device(here.z, x, y, here.l)

    barrier = pltpu.get_barrier_semaphore()
    peers = [partner(r)[1] for r in range(1, plane)] + [here.z_peer(k) for k in range(1, nz)]
    if extras:
        peers += [here.low_peer(k) for k in range(1, here.nl)]
    for peer in peers:
        pl.semaphore_signal(barrier, inc=1, device_id=peer, device_id_type=pl.DeviceIdType.MESH)
    pl.semaphore_wait(barrier, len(peers))

    def to_near(r):
        at, peer = partner(r)
        return remote(part_ref.at[:, at], near.at[r - 1], near_sems.at[r, 0], near_sems.at[r, 1], peer)

    def to_far(k):
        return remote(sent.at[here.z_after(k)], far.at[k - 1], far_sems.at[k, 0], far_sems.at[k, 1], here.z_peer(k))

    def back_far(k, z):
        return remote(res, out_ref.at[z, spot], back_sems.at[k, 0], back_sems.at[k, 1], here.z_peer(k))

    def back_near(r, at):
        src = out_ref.at[:, spot]
        return remote(src, out_ref.at[:, at], wide_sems.at[r, 0], wide_sems.at[r, 1], partner(r)[1])

    def swaps(k):
        to = here.low_after(k)
        return [
            remote(src.at[:, to], dst.at[k - 1], pairs.at[k, n, 0], pairs.at[k, n, 1], here.low_peer(k))
            for n, (src, dst) in enumerate(zip(extra_in[1:], extra_out[1:]))
        ]

    for r in range(1, plane):
        to_near(r).start()
    for r in range(1, plane):
        to_near(r).wait_recv()

    def total(z):
        out = part_ref[z, spot].astype(F32)
        for r in range(1, plane):
            out = out + near[r - 1, z].astype(F32)
        return out

    for k in range(1, nz):
        z = here.z_after(k)
        sent[z] = total(z).astype(BF16)
        to_far(k).start()
    if extras:
        column = Columns(here, extra_in[0], columns)
        column.begin()
    mine = total(here.z)
    for k in range(1, nz):
        to_far(k).wait_recv()
        mine = mine + far[k - 1].astype(F32)
    res[...] = mine.astype(BF16)
    own = pltpu.make_async_copy(res, out_ref.at[here.z, spot], keep.at[0])
    own.start()
    for k in range(1, nz):
        back_far(k, here.z).start()
    own.wait()
    for k in range(1, nz):
        back_far(k, here.z_before(k)).wait_recv()
    for r in range(1, plane):
        back_near(r, spot).start()
    if extras:

        def merge(n, carry):
            extra_out[0][here.after(n)] = column.merged(n)
            return carry

        lax.fori_loop(0, here.groups, merge, 0)
    for r in range(1, plane):
        back_near(r, partner(r)[0]).wait()
        to_near(r).wait_send()
    for k in range(1, nz):
        to_far(k).wait_send()
        back_far(k, here.z).wait_send()
    if extras:
        column.end()
        for k in range(1, here.nl):
            for copy in swaps(k):
                copy.wait()


def share(dims, name_id, part, extras=()):
    ns, ny, nl = dims
    nz, plane = ns // NX, NX * ny
    shape = jax.ShapeDtypeStruct
    block = (XCOLS, MBLK)
    far = [shape((nl - 1, e.shape[0]) + e.shape[2:], F32) for e in extras[1:]]
    far_specs = [any_spec()] * len(far)
    if extras:
        far = [shape((ns * ny, MODES) + extras[0].shape[3:], BF16)] + far
        far_specs = [vmem_spec()] + far_specs
    return pl.pallas_call(
        functools.partial(share_kernel, dims, len(extras)),
        in_specs=[vmem_spec()] + [any_spec()] * len(extras),
        out_specs=[any_spec()] + far_specs,
        out_shape=[shape((nz, plane) + block, BF16)] + far,
        scratch_shapes=[
            VMEM((plane - 1, nz) + block, BF16), VMEM((nz,) + block, BF16), VMEM((nz - 1,) + block, BF16),
            VMEM(block, BF16), DMA((plane, 2)), DMA((nz, 2)), DMA((nz, 2)), DMA((plane, 2)), DMA((1,)),
            DMA((nl, max(len(extras), 1), 2)),
        ]
        + (column_scratch(dims, extras[0].shape[3], extras[0].shape[4]) if extras else []),
        compiler_params=comm_params(name_id, 60),
        cost_estimate=comm_cost(30),
        name="share",
    )(part.reshape((nz, plane) + block), *extras)


class Staged:
    def __init__(self, dims, parts):
        self.ns, self.ny, _ = dims
        self.nz = self.ns // NX
        self.parts = parts
        self.z = lax.axis_index("seq") // NX

    def plane(self):
        out = []
        for r in range(1, NX * self.ny):
            dx, dy = r // self.ny, r % self.ny
            moves = []
            for g in range(self.ns * self.ny):
                z, x, y = g // self.ny // NX, g // self.ny % NX, g % self.ny
                moves.append((g, (z * NX + (x + dx) % NX) * self.ny + (y + dy) % self.ny))
            out.append(lax.ppermute(self.parts[r], GROUP, moves))
        return out

    def line(self, got):
        total = self.parts[0].astype(F32)
        for piece in got:
            total = total + piece.astype(F32)
        return total.astype(BF16)

    def along(self, line):
        out = [lax.dynamic_index_in_dim(line, self.z, 0, keepdims=False)]
        for k in range(1, self.nz):
            moves = [(s, ((s // NX + k) % self.nz) * NX + s % NX) for s in range(self.ns)]
            piece = lax.dynamic_index_in_dim(line, (self.z + k) % self.nz, 0, keepdims=False)
            out.append(lax.ppermute(piece, "seq", moves))
        return out


def exit_kernel(
    dims, modes_ref, joint_ref, w_ref, ing_ref, dtg_ref, outg_ref, xg_ref, suma_ref, sumb_ref,
    x_ref, cot_ref, gain_ref, pick_ref,
    grad_out, gsum_out, ing_out, dtg_out, outg_out, xg_out, suma_out, sumb_out,
    part_ref, gparts, gslots, ready, pairs, smalls, cols, *bufs,
):
    here = Place(dims)
    rows_d, chan = ing_ref.shape[3], ing_ref.shape[4]
    rows_e = dtg_ref.shape[2]
    more = len(column_scratch(dims, 16, 128))
    columns, bufs = bufs[:more], bufs[more:]
    greet_all(here)
    nz, plane = here.nz, NX * here.ny
    reduce = Reduce(here, part_ref, MBLK, bufs, False)
    column = Columns(here, ing_ref, columns)

    def landing(g):
        return ing_out.at[:, :, pl.ds(pl.multiple_of(g * chan, chan), chan)]

    def col_copy(n, g):
        return remote(ready.at[n], landing(g), cols.at[n, 0], cols.at[n, 1], here.of_group(here.after(n), here.l))

    def own_copy():
        return pltpu.make_async_copy(ready.at[0], landing(here.g), cols.at[0, 0])

    def send_inner(n, carry):
        ready[n] = column.merged(n)
        col_copy(n, here.g).start()
        return carry

    def pair_copies(k):
        to = here.low_after(k)
        peer = here.low_peer(k)
        out = []
        for n, (src, dst) in enumerate(((dtg_ref, dtg_out), (outg_ref, outg_out))):
            out.append(remote(src.at[:, to], dst.at[k - 1], pairs.at[k, n, 0], pairs.at[k, n, 1], peer))
        for n, (src, dst) in enumerate(((xg_ref, xg_out), (suma_ref, suma_out), (sumb_ref, sumb_out))):
            sems = pairs.at[k, n + 2]
            out.append(remote(lanes_at(src, to, rows_e), dst.at[k - 1], sems.at[0], sems.at[1], peer))
        return out

    def first(k):
        z = reduce.target(k)

        def one(p, carry):
            x, y = lax.div(p, here.ny), lax.rem(p, here.ny)
            block = here.group(z, x, y)
            product = nt_dot(joint_ref[block], w_ref[modes_ref[block]])
            part_ref[z, x, y] = product.astype(BF16)
            return carry

        lax.fori_loop(0, plane, one, 0)
        reduce.first(k)

    first(0)
    first(1)
    column.begin()
    for k in range(nz):
        if k + 2 < nz:
            first(k + 2)
        if k == 1:
            for low in range(1, here.nl):
                for copy in pair_copies(low):
                    copy.start()
        reduce.second(k)
        if k > 0:
            reduce.third(k - 1)
        lax.fori_loop(max(k * plane, 1), (k + 1) * plane, send_inner, 0)
    ready[0] = column.merged(0)
    own_copy().start()
    reduce.last()

    acc = reduce.acc
    x = x_ref[...].astype(F32)
    scale = lax.rsqrt(jnp.mean(x * x, -1, keepdims=True) + NORM_EPS)
    back = acc[...]
    weighted = back * gain_ref[0:1, :]
    dots = jnp.mean(weighted * x, -1, keepdims=True)
    back_x = scale * weighted - x * (scale * scale * scale) * dots
    grad_out[...] = (cot_ref[...].astype(F32) + back_x).astype(BF16)
    felt = jnp.sum(back * x * scale, 0, keepdims=True)
    for t in range(D // 128):
        gparts[t] = felt[:, t * 128 : (t + 1) * 128] * pick_ref[...]

    def small_copy(k):
        i = lax.rem(here.i + k, here.devices)
        src = gparts.at[lax.div(i * rows_d, 128)]
        return remote(src, gslots.at[here.i], smalls.at[k, 0], smalls.at[k, 1], here.of_index(i))

    def send_small(k, carry):
        small_copy(k).start()
        return carry

    lax.fori_loop(1, here.devices, send_small, 0)
    gslots[here.i] = gparts[lax.div(here.i * rows_d, 128)]
    reduce.end()
    column.end()
    for k in range(1, here.nl):
        for copy in pair_copies(k):
            copy.wait()
    own_copy().wait()

    def end_cols(n, carry):
        col_copy(n, here.before(n)).wait()
        return carry

    lax.fori_loop(1, here.groups, end_cols, 0)

    def end_small(k, carry):
        small_copy(k).wait()
        return carry

    lax.fori_loop(1, here.devices, end_small, 0)
    gsum_out[...] = jnp.sum(gslots[...], 0)


def leave(dims, modes, joint, w_in, ing, swapped, rest, x, cot, gain, pick):
    ns, ny, nl = dims
    groups, devices = ns * ny, ns * ny * nl
    shape = jax.ShapeDtypeStruct
    rows_d, chan, rows_e = ing.shape[3], ing.shape[4], swapped[0].shape[2]
    return pl.pallas_call(
        functools.partial(exit_kernel, dims),
        in_specs=[pl.BlockSpec(memory_space=pltpu.SMEM)] + [vmem_spec()] * 2 + [any_spec()] * 6 + [vmem_spec()] * 4,
        out_specs=[vmem_spec()] * 2 + [any_spec()] * 6,
        out_shape=[
            shape((MBLK, D), BF16), shape((8, 128), F32), shape((MODES, rows_d, INNER), BF16),
            *[shape((nl - 1, MODES) + part.shape[2:], F32) for part in swapped],
            *[shape((nl - 1, part.shape[-2], rows_e), F32) for part in rest],
        ],
        scratch_shapes=[
            VMEM((ns // NX, NX, ny, MBLK, D), BF16),
            VMEM((D // 128, 8, 128), F32), VMEM((devices, 8, 128), F32), VMEM((groups, MODES, rows_d, chan), BF16),
            DMA((nl, 5, 2)), DMA((devices, 2)), DMA((groups, 2)),
            *column_scratch(dims, rows_d, chan),
            *reduce_scratch(dims, MBLK, D, BF16),
        ],
        compiler_params=comm_params(4, 63),
        cost_estimate=comm_cost(100),
        name="leave",
    )(modes, joint, w_in, ing, *swapped, *rest, x, cot, gain, pick)


def body(
    tokens, modality, cotangent, in_weight, x_weight, dt_weight, out_weight, norm_gain, channel_params,
    in_first, in_second, x_first, x_second, dt_first, dt_second, out_first, out_second,
    gain_first, gain_second, chan_first, chan_second,
):
    nb, seqs, los = lax.axis_size("seq"), lax.axis_size("hi"), lax.axis_size("lo")
    dims = (nb, seqs, los)
    groups = nb * seqs
    chan = INNER // groups
    rows_d = in_weight.shape[0]
    rows_e = x_weight.shape[0]
    plan = Plan(nb, seqs, chan)
    low = lax.axis_index("lo")
    index = (lax.axis_index("seq") * seqs + lax.axis_index("hi")) * los + low
    lane = lax.rem(index * rows_d, 128)

    mode_here = modality[0, 0]
    small = jnp.zeros((8, 128), F32)
    small = lax.dynamic_update_slice(small, rounded(norm_gain.T), (0, lane))
    small = small.at[MODES].set(mode_here.astype(F32))
    pick = (mode_here == lax.broadcasted_iota(jnp.int32, (8, 128), 0)).astype(F32)

    in_cols = in_weight.astype(BF16).swapaxes(0, 1)
    x_low = x_weight.astype(BF16).transpose(1, 2, 0).reshape(MODES * XCOLS, rows_e)
    dt_low = dt_weight.astype(BF16).swapaxes(0, 1)
    out_low = out_weight.astype(BF16).swapaxes(0, 1)
    chan_low = jnp.pad(rounded(channel_params).T, ((0, PAR_ROWS - channel_params.shape[1]), (0, 0)))
    mode_row, gain, normal, w_in, w_dt, w_out, w_x, par = entry(
        dims, small, pick, tokens[0], in_cols, dt_low, out_low, x_low, chan_low
    )
    modes = mode_row[0, :groups].astype(jnp.int32)
    w_x = lanes_join(w_x).reshape(MODES, XCOLS, chan)
    par = lanes_join(par)
    rates = -jnp.exp(par[PAR_RATES : PAR_RATES + STATE])
    rates_f = plan.fold_rates(rates / LN2)
    select = jnp.asarray(plan.select(), BF16)

    cot_here, _ = lax.optimization_barrier((cotangent[0], gain))
    cot = lax.all_gather(cot_here, GROUP, axis=0)

    inner, gate, pre, act, proj_part = front(plan, modes, normal, w_in, w_x, par)
    (proj,) = share(dims, 2, proj_part)
    proj = proj.reshape(groups, XCOLS, MBLK)
    spot = jnp.stack([lax.axis_index("seq") % NX, lax.axis_index("hi")]).astype(jnp.int32)
    scanned, mixed, before, last, *out_parts = forward_scan(
        plan, jnp.concatenate([modes, spot]), proj, act, gate, w_dt, w_out, par, rates_f, select
    )
    staged = Staged(dims, out_parts)
    crossed = staged.plane()

    bact, bgate, bproj_part, dt_g, out_g, gate_g, sums_a = backward_scan(
        plan, modes, cot, normal, proj, act, gate, scanned, mixed, before, last, w_dt, w_out, par, rates_f, select
    )
    dt_g = dt_g.reshape(MODES, los, rows_e, RANK)
    out_g = out_g.reshape(MODES, los, rows_e, D)
    gate_g = gate_g.reshape(MODES, groups, los, rows_d, chan)
    crossed, bproj_part = lax.optimization_barrier((crossed, bproj_part))
    bproj, gate_ready = share(dims, 3, bproj_part, (gate_g,))
    bproj = bproj.reshape(groups, XCOLS, MBLK)
    gate_grad = lax.all_to_all(gate_ready, GROUP, 0, 0)
    joint, in_g, x_g, sums_b = tail(
        plan, modes, bproj, bact, bgate, pre, act, inner, normal, w_x, par
    )
    rest = (x_g.reshape(MODES * XCOLS, chan), sums_a, sums_b)
    input_grad, gain_sum, inner_grad, dt_far, out_far, *rest_far = leave(
        dims, modes, joint, w_in, in_g.reshape(MODES, groups, los, rows_d, chan), (dt_g, out_g),
        tuple(lanes_split(part, los) for part in rest), tokens[0], cotangent[0], gain, pick,
    )

    crossed, gain_sum = lax.optimization_barrier((crossed, gain_sum))
    pieces = staged.along(staged.line(crossed))

    def merged(near, far):
        return lax.dynamic_index_in_dim(near, low, 1, keepdims=False) + jnp.sum(far, 0)

    gate_grad = gate_grad.transpose(2, 1, 0, 3).reshape(rows_d, MODES, INNER)
    in_grad = jnp.concatenate([inner_grad.swapaxes(0, 1), gate_grad], 2).astype(F32)
    dt_grad = merged(dt_g, dt_far).swapaxes(0, 1)
    out_grad = merged(out_g, out_far).swapaxes(0, 1)
    x_sum, sum_a, sum_b = (
        lax.dynamic_slice_in_dim(near, low * rows_e, rows_e, 1) + jnp.sum(far, 0) for near, far in zip(rest, rest_far)
    )
    x_grad = x_sum.reshape(MODES, XCOLS, rows_e).transpose(2, 0, 1)
    chan_grad = jnp.concatenate(
        [
            sum_a[:MODES],
            sum_b[CONV : CONV + 1],
            sum_a[MODES : MODES + 1],
            sum_b[:CONV],
            sum_a[SUM_LOG:],
        ],
        0,
    ).T
    gain_grad = lax.dynamic_slice(gain_sum, (0, lane), (MODES, rows_d)).T

    in_new = adam_update(in_weight, in_first, in_second, in_grad, D ** (-0.5))
    x_new = adam_update(x_weight, x_first, x_second, x_grad, INNER ** (-0.5))
    dt_new = adam_update(dt_weight, dt_first, dt_second, dt_grad, RANK ** (-0.5))
    out_new = adam_update(out_weight, out_first, out_second, out_grad, (4 * INNER) ** (-0.5))
    gain_new = adam_update(norm_gain, gain_first, gain_second, gain_grad, SMALL_RATE)
    chan_new = adam_update(channel_params, chan_first, chan_second, chan_grad, CHAN_RATE)
    pieces, in_new = lax.optimization_barrier((pieces, in_new))
    out_sum = tokens[0].astype(F32)
    for piece in pieces:
        out_sum = out_sum + piece.astype(F32)
    block_out = out_sum.astype(BF16)[None]
    return (
        block_out,
        input_grad[None],
        *in_new,
        in_new[0].astype(BF16),
        *x_new,
        x_new[0].astype(BF16),
        *dt_new,
        dt_new[0].astype(BF16),
        *out_new,
        out_new[0].astype(BF16),
        *gain_new,
        *chan_new,
    )


def solution(mesh):
    seq, batch = mesh.shape["seq"], mesh.shape["batch"]
    high = max(1, min(batch, GROUPS // seq))
    split = Mesh(mesh.devices.reshape(seq, high, batch // high), EVERY)
    token = P(("hi", "lo"), "seq", None)
    wide = P(EVERY, None, None)
    flat = P(EVERY, None)
    return jax.shard_map(
        body,
        mesh=split,
        in_specs=(token, P(("hi", "lo"), "seq"), token) + (wide,) * 4 + (flat,) * 2 + (wide,) * 8 + (flat,) * 4,
        out_specs=(token,) * 2 + (wide,) * 16 + (flat,) * 6,
        check_vma=False,
    )
```

time: 7700 us -> 636 us (0.08)
  waiting for transfers between devices: 3550 us -> 71.1 us
  local copies, waits for them, and re-layouts: 2230 us -> 6.52 us
  other arithmetic: 1610 us -> 51.6 us
  Pallas kernels: 0 us -> 476 us
  matrix products: 113 us -> 0 us
    reduce_scatter x4 -> x0, waiting for transfers between devices: 2650 us -> none  [the longest x1 1420 us: body(): lax.psum_scatter(mode_grads((normal_low,), (joint_low,), block_modes, lax...]
    pad x296 -> x1, local copies, waits for them, and re-layouts: 1760 us -> 0.61 us  [body(): jnp.pad(rounded(channel_params).T, ((0, PAR_ROWS - channel_params.shape[1...]
    all_gather x7 -> x1, waiting for transfers between devices: 827 us -> 32.6 us  [body(): cot = lax.all_gather(cot_here, GROUP, axis=0)]
    mul x122 -> x0, other arithmetic: 576 us -> none  [the longest x104 495 us: combine_maps(): return (earlier[0] * later[0], later[0] * earlier[1] + later[1])]
    pallas_call x0 -> x8, Pallas kernels: none -> 476 us  [the longest x1 144 us: leave(): pl.pallas_call(functools.partial(exit_kernel, dims), in_specs=[pl.BlockSp...]
    add x116 -> x6, other arithmetic: 349 us -> 17.9 us  [the longest x1 11.4 us: adam_update(): second_new = BETA_TWO * second + (1.0 - BETA_TWO) * grad * grad]
    reduce_sum x21 -> x0, other arithmetic: 198 us -> none  [the longest x8 108 us: scan_piece(): return (states[-1], jnp.sum(states * leave[:, :, None], 1))]
    while x650 -> x0, local copies, waits for them, and re-layouts: 195 us -> none
  transfers between devices with their start and end apart: 14 -> 8, of which waited for: 11 -> 4; matrix products, arithmetic and copies ran while one was open for 11% -> 6% of each run, Pallas kernels for 0% -> 26%
where the time goes in v1:
time: 636 us; the launch traced here: 635 us
  Pallas kernels  476 us (75%)
  waiting for transfers between devices  71.1 us (11%)
  other arithmetic  51.6 us (8%)
  between operations  15.1 us (2%)
  starting transfers between devices  14.4 us (2%)
  local copies, waits for them, and re-layouts  6.52 us (1%)
    pallas_call x1, Pallas kernels, leave(): pl.pallas_call(functools.partial(exit_kernel, dims), in_specs=[pl.BlockSp...  144 us
    pallas_call x1, Pallas kernels, entry(): pl.pallas_call(functools.partial(entry_kernel, dims), in_specs=[vmem_spec...  118 us
    pallas_call x1, Pallas kernels, backward_scan(): pl.pallas_call(functools.partial(back_kernel, plan), grid_spec=pltpu.Pref...  73.3 us
    pallas_call x2, Pallas kernels, share(): pl.pallas_call(functools.partial(share_kernel, dims, len(extras)), in_spe...  71.4 us
    pallas_call x1, Pallas kernels, forward_scan(): pl.pallas_call(functools.partial(scan_kernel, plan), grid_spec=pltpu.Pref...  36.6 us
    all_gather x1, waiting for transfers between devices, body(): cot = lax.all_gather(cot_here, GROUP, axis=0)  32.6 us
    all_to_all x1, waiting for transfers between devices, body(): gate_grad = lax.all_to_all(gate_ready, GROUP, 0, 0)  31 us
    pallas_call x1, Pallas kernels, tail(): pl.pallas_call(functools.partial(tail_kernel, plan), grid_spec=pltpu.Pref...  17.8 us
  transfers between devices with their start and end apart: 8, of which 4 were waited for; matrix products, arithmetic and copies ran while one was open for 6% of the time, Pallas kernels for 26%

profile of v1, /device:TPU:10, one launch (start us, length us, event | category | flops | bytes accessed | tf_op | source)
XLA Modules:
  0.0 634.9 jit_solution(5777281399582665668)
XLA Ops:
  9.2 5.0 convert_bitcast_fusion.win_ref
  18.5 118.1 %entry.1 = (f32[8,128]{1,0:T(8,128)}, f32[8,2048]{1,0:T(8,128)}, bf16[16,128,2048]{2,1,0:T(8,128)(2,1)}, bf16[3,2048,512]{2,1,0:T(8,128)(2,1)}, bf16[3,256,128]{...) custom-call(f32[8,128]{1,0:T(8,128)} %copy-done.18, ...), custom_call_target="tpu_custom_call" | custom-call | bytes 300000000 | tf_op jit(solution)/shard_map/entry/pallas_call | solution.py:1251
  137.9 15.4 %front.1 = (bf16[16,128,256]{2,1,0:T(8,128)(2,1)}, f32[16,128,256]{2,1,0:T(8,128)}, f32[16,128,256]{2,1,0:T(8,128)}, bf16[16,128,256]{2,1,0:T(8,128)(2,1)}, bf16[16,160,128]{2,1,0:T(8,128)(2,1)}) custom-call(s32[16]{0:T(128)} %convert_bitcast_fusion.3.modes.modes_ref, bf16[16,128,2048]{2,1,0:T(8,128)(2,1)} %get-tuple-element.95.x_ref, ...), custom_call_target="tpu_custom_call" | custom-call | flops 4294967296 | bytes 25165824 | tf_op jit(solution)/shard_map/front/pallas_call | solution.py:184
  153.3 39.9 %share.2 = bf16[4,4,160,128]{3,2,1,0:T(8,128)(2,1)} custom-call(bf16[4,4,160,128]{3,2,1,0:T(8,128)(2,1)} %bitcast.128), custom_call_target="tpu_custom_call" | custom-call | bytes 90000000 | tf_op jit(solution)/shard_map/share/pallas_call | solution.py:1423
  194.5 36.6 %forward_scan.1 = (f32[16,128,256]{2,1,0:T(8,128)}, bf16[16,128,256]{2,1,0:T(8,128)(2,1)}, f32[1024,8,8,128]{3,2,1,0:T(8,128)}, f32[8,8,128]{2,1,0:T(8,128)}, bf...) custom-call(s32[18]{0:T(128)} %pad_add_fusion.modes, ...), custom_call_target="tpu_custom_call" | custom-call | flops 503316480 | bytes 157286400 | tf_op jit(solution)/shard_map/forward_scan/pallas_call | solution.py:299
  234.7 32.6 %all-gather.3.cloned.1.call-done = bf16[2048,2048]{1,0:T(8,128)(2,1)} async-done(((bf16[128,2048]{1,0:T(8,128)(2,1)}), bf16[2048,2048]{1,0:T(8,128)(2,1)}) %all-gather.3.cloned.1.call-update) | async-done | bytes 8388624 | tf_op jit(solution)/shard_map/all_gather | solution.py:1654
  267.3 73.3 %backward_scan.1 = (f32[16,128,256]{2,1,0:T(8,128)}, bf16[16,128,256]{2,1,0:T(8,128)(2,1)}, bf16[16,160,128]{2,1,0:T(8,128)(2,1)}, f32[3,256,128]{2,1,0:T(8,128)...) custom-call(s32[16]{0:T(128)} %convert_bitcast_fusion.3.modes.modes_ref, ...), custom_call_target="tpu_custom_call" | custom-call | flops 838860800 | bytes 314572800 | tf_op jit(solution)/shard_map/backward_scan/pallas_call | solution.py:488
  340.6 31.5 %share.3 = (bf16[4,4,160,128]{3,2,1,0:T(8,128)(2,1)}, bf16[16,3,64,256]{3,2,1,0:T(8,128)(2,1)}) custom-call(bf16[4,4,160,128]{3,2,1,0:T(8,128)(2,1)} %bitcast.129, f32[3,16,2,64,256]{4,3,2,1,0:T(8,128)} %bitcast.114), custom_call_target="tpu_custom_call" | custom-call | bytes 90000000 | tf_op jit(solution)/shard_map/share/pallas_call | solution.py:1423
  372.1 17.8 %tail.1 = (bf16[16,128,512]{2,1,0:T(8,128)(2,1)}, f32[3,2048,256]{2,1,0:T(8,128)}, f32[3,160,256]{2,1,0:T(8,128)}, f32[8,256]{1,0:T(8,128)}) custom-call(s32[16]{0:T(128)} %convert_bitcast_fusion.3.modes.modes_ref, bf16[16,160,128]{2,1,0:T(8,128)(2,1)} %bitcast.135, f32[16,128,256]{2,1,0:T(8,128)} %get-tuple-element.121.bact_ref, ...), custom_call_target="tpu_custom_call" | custom-call | flops 8589934592 | bytes 41943040 | tf_op jit(solution)/shard_map/tail/pallas_call | solution.py:579
  389.9 143.7 %leave.1 = (bf16[128,2048]{1,0:T(8,128)(2,1)}, f32[8,128]{1,0:T(8,128)}, bf16[3,64,4096]{2,1,0:T(8,128)(2,1)}, f32[1,3,128,128]{3,2,1,0:T(8,128)}, f32[1,3,128,2...) custom-call(s32[16]{0:T(128)} %convert_bitcast_fusion.3.modes.modes_ref, ...), custom_call_target="tpu_custom_call" | custom-call | bytes 300000000 | tf_op jit(solution)/shard_map/leave/pallas_call | solution.py:1594
  535.2 6.4 %all-to-all-start = ((bf16[16,3,64,256]{3,2,1,0:T(8,128)(2,1)}), bf16[16,3,64,256]{3,2,1,0:T(8,128)(2,1)}, u32[]{:S(2)}, u32[]{:S(2)}) async-start(bf16[16,3,64,256]{3,2,1,0:T(8,128)(2,1)} %get-tuple-element.137), calls=%async_computation | async-start | bytes 3145728 | tf_op jit(solution)/shard_map/all_to_all | solution.py:1675
  541.6 4.6 add_convert_fusion
  555.0 2.2 fusion.14
  557.2 1.6 broadcast_multiply_fusion.2
  558.8 2.2 fusion.16
  561.0 7.8 %fusion.12 = (bf16[128,3,2048]{2,0,1:T(8,128)(2,1)}, f32[128,3,2048]{2,0,1:T(8,128)}, f32[128,3,2048]{2,0,1:T(8,128)}, f32[3,128,2048]{2,1,0:T(8,128)S(1)}) fusion(f32[128,3,2048]{2,0,1:T(8,128)S(1)} %copy-done.2, f32[128,3,2048]{2,0,1:T(8,128)} %param.41, f32[128,3,2048]{2,0,1:T(8,128)} %param.42, f32[1,3,128,2048]{3,2,1,0:T(8,128)} %get-tuple-element.148, ...), kind=kLoop, calls=%fused_computation.53 | loop fusion | flops 11796480 | bytes 26738692 | tf_op jit(solution)/shard_map/convert_element_type | solution.py:1732
  568.8 2.2 broadcast_multiply_fusion
  571.1 31.0 %all-to-all-done = bf16[16,3,64,256]{3,2,1,0:T(8,128)(2,1)} async-done(((bf16[16,3,64,256]{3,2,1,0:T(8,128)(2,1)}), bf16[16,3,64,256]{3,2,1,0:T(8,128)(2,1)}, u32[]{:S(2)}, u32[]{:S(2)}) %all-to-all-start) | async-done | bytes 1572896 | tf_op jit(solution)/shard_map/all_to_all | solution.py:1675
  602.1 1.6 copy.50
  603.7 11.4 %fusion = (f32[64,3,8192]{2,0,1:T(8,128)}, f32[64,3,8192]{2,0,1:T(8,128)S(1)}, f32[64,3,8192]{2,0,1:T(8,128)}) fusion(f32[64,3,8192]{2,0,1:T(8,128)} %param.36, bf16[64,3,4096]{2,0,1:T(8,128)(2,1)S(1)} %bitcast.113, bf16[64,3,4096]{2,0,1:T(8,128)(2,1)S(1)} %bitcast.122, f32[64,3,8192]{2,0,1:T(8,128)} %param.29, f32[64,3,8192]{2,0,1:T(8,128)} %param.35), kind=kLoop, calls=%fused_computation.2 | loop fusion | flops 28311552 | bytes 40894464 | tf_op jit(solution)/shard_map/add | solution.py:42
  615.1 5.5 collective-permute-done.4
  620.6 1.9 collective-permute-done.5
  622.6 2.1 convert_element_type.93
  624.6 2.6 fusion.3
  (91 shorter events, 22.7 us)
Async XLA Ops:
  7.2 260.1 %all-gather.3.cloned.1.call-start = ((), (), s32[]{:S(2)}) async-start(), calls=%async_computation.1 | async-start | bytes 8912896 | tf_op jit(solution)/shard_map/all_gather | solution.py:1654
  137.8 55.3 %copy-start.12 = (f32[32,256]{1,0:T(8,128)S(1)}, f32[32,256]{1,0:T(8,128)}, u32[]{:S(2)}) copy-start(f32[32,256]{1,0:T(8,128)} %get-tuple-element.98.par_ref) | copy-start | bytes 98308
  137.8 55.4 %copy-start.20 = (s32[16]{0:T(128)S(1)}, s32[16]{0:T(128)}, u32[]{:S(2)}) copy-start(s32[16]{0:T(128)} %convert_bitcast_fusion.3.modes.modes_ref) | copy-start | bytes 196
  231.1 109.4 %collective-permute-start = (bf16[4,128,2048]{2,1,0:T(8,128)(2,1)}, bf16[4,128,2048]{2,1,0:T(8,128)(2,1)S(1)}, u32[]{:S(2)}, u32[]{:S(2)}) collective-permute-start(bf16[4,128,2048]{2,1,0:T(8,128)(2,1)} %get-tuple-element.105), channel_id=1, source_target_pairs={{0,2},{2,0},{4,6},{6,4},{8,10},{10,8},{12,14},{14,12},{16,18},{18,... | collective-permute-start | bytes 6291464 | tf_op jit(solution)/shard_map/ppermute | solution.py:1455
  231.8 108.8 %collective-permute-start.1 = (bf16[4,128,2048]{2,1,0:T(8,128)(2,1)}, bf16[4,128,2048]{2,1,0:T(8,128)(2,1)}, u32[]{:S(2)}, u32[]{:S(2)}) collective-permute-start(bf16[4,128,2048]{2,1,0:T(8,128)(2,1)} %get-tuple-element.106), channel_id=1, source_target_pairs={{0,4},{2,6},{4,0},{6,2},{8,12},{10,14},{12,8},{14,10},{16,20},{18,... | collective-permute-start | bytes 6291464 | tf_op jit(solution)/shard_map/ppermute | solution.py:1455
  233.2 107.4 %collective-permute-start.2 = (bf16[4,128,2048]{2,1,0:T(8,128)(2,1)}, bf16[4,128,2048]{2,1,0:T(8,128)(2,1)}, u32[]{:S(2)}, u32[]{:S(2)}) collective-permute-start(bf16[4,128,2048]{2,1,0:T(8,128)(2,1)} %get-tuple-element.107), channel_id=1, source_target_pairs={{0,6},{2,4},{4,2},{6,0},{8,14},{10,12},{12,10},{14,8},{16,22},{18,... | collective-permute-start | bytes 6291464 | tf_op jit(solution)/shard_map/ppermute | solution.py:1455
  340.6 31.5 %copy-start.6 = (bf16[4,128,2048]{2,1,0:T(8,128)(2,1)}, bf16[4,128,2048]{2,1,0:T(8,128)(2,1)S(1)}, u32[]{:S(2)}) copy-start(bf16[4,128,2048]{2,1,0:T(8,128)(2,1)S(1)} %collective-permute-done) | copy-start | bytes 6291460
  389.9 143.7 %copy-start.15 = (f32[8,256]{1,0:T(8,128)S(1)}, f32[8,256]{1,0:T(8,128)}, u32[]{:S(2)}) copy-start(f32[8,256]{1,0:T(8,128)} %get-tuple-element.131.sumb_ref) | copy-start | bytes 24580
  389.9 144.6 %copy-start.14 = (f32[24,256]{1,0:T(8,128)S(1)}, f32[24,256]{1,0:T(8,128)}, u32[]{:S(2)}) copy-start(f32[24,256]{1,0:T(8,128)} %get-tuple-element.130.suma_ref) | copy-start | bytes 73732
  533.6 8.0 %copy-start.5 = (bf16[4,128,2048]{2,1,0:T(8,128)(2,1)S(1)}, bf16[4,128,2048]{2,1,0:T(8,128)(2,1)}, u32[]{:S(2)}) copy-start(bf16[4,128,2048]{2,1,0:T(8,128)(2,1)} %get-tuple-element.104) | copy-start | bytes 6291460
  535.2 66.8 %all-to-all-start = ((bf16[16,3,64,256]{3,2,1,0:T(8,128)(2,1)}), bf16[16,3,64,256]{3,2,1,0:T(8,128)(2,1)}, u32[]{:S(2)}, u32[]{:S(2)}) async-start(bf16[16,3,64,256]{3,2,1,0:T(8,128)(2,1)} %get-tuple-element.137), calls=%async_computation | async-start | bytes 3145728 | tf_op jit(solution)/shard_map/all_to_all | solution.py:1675
  546.2 6.3 copy-start.16
  546.2 6.3 copy-start.17
  546.3 6.9 %copy-start.19 = (f32[64,3]{0,1:T(4,128)S(1)}, f32[64,3]{0,1:T(4,128)}, u32[]{:S(2)}) copy-start(f32[64,3]{0,1:T(4,128)} %param.33) | copy-start | bytes 2308
  546.3 6.9 %copy-start.21 = (f32[64,3]{0,1:T(4,128)S(1)}, f32[64,3]{0,1:T(4,128)}, u32[]{:S(2)}) copy-start(f32[64,3]{0,1:T(4,128)} %param.43) | copy-start | bytes 2308
  546.3 6.9 %copy-start.22 = (f32[64,3]{0,1:T(4,128)S(1)}, f32[64,3]{0,1:T(4,128)}, u32[]{:S(2)}) copy-start(f32[64,3]{0,1:T(4,128)} %param.44) | copy-start | bytes 2308
  546.3 6.9 %copy-start.23 = (f32[8,128]{1,0:T(8,128)S(1)}, f32[8,128]{1,0:T(8,128)}, u32[]{:S(2)}) copy-start(f32[8,128]{1,0:T(8,128)} %get-tuple-element.149) | copy-start | bytes 12292
  547.7 13.3 %copy-start.2 = (f32[128,3,2048]{2,0,1:T(8,128)S(1)}, f32[128,3,2048]{2,0,1:T(8,128)}, u32[]{:S(2)}) copy-start(f32[128,3,2048]{2,0,1:T(8,128)} %param.32) | copy-start | bytes 9437188
  547.7 67.4 %collective-permute-start.3 = (bf16[128,2048]{1,0:T(8,128)(2,1)}, bf16[128,2048]{1,0:T(8,128)(2,1)}, u32[]{:S(2)}, u32[]{:S(2)}) collective-permute-start(bf16[128,2048]{1,0:T(8,128)(2,1)} %get-tuple-element.172), channel_id=1, source_target_pairs={{0,8},{4,12},{8,16},{12,20},{16,24},{20,28},{24,0},{28,4},{1,9},{5... | collective-permute-start | bytes 1572872 | tf_op jit(solution)/shard_map/ppermute | solution.py:1469
  549.2 71.5 %collective-permute-start.4 = (bf16[128,2048]{1,0:T(8,128)(2,1)}, bf16[128,2048]{1,0:T(8,128)(2,1)}, u32[]{:S(2)}, u32[]{:S(2)}) collective-permute-start(bf16[128,2048]{1,0:T(8,128)(2,1)} %get-tuple-element.171), channel_id=1, source_target_pairs={{0,16},{4,20},{8,24},{12,28},{16,0},{20,4},{24,8},{28,12},{1,17},{... | collective-permute-start | bytes 1572872 | tf_op jit(solution)/shard_map/ppermute | solution.py:1469
  550.6 72.0 %collective-permute-start.5 = (bf16[128,2048]{1,0:T(8,128)(2,1)}, bf16[128,2048]{1,0:T(8,128)(2,1)}, u32[]{:S(2)}, u32[]{:S(2)}) collective-permute-start(bf16[128,2048]{1,0:T(8,128)(2,1)} %get-tuple-element.170), channel_id=1, source_target_pairs={{0,24},{4,28},{8,0},{12,4},{16,8},{20,12},{24,16},{28,20},{1,25},{... | collective-permute-start | bytes 1572872 | tf_op jit(solution)/shard_map/ppermute | solution.py:1469
  561.0 7.8 %copy-start.3 = (f32[128,3,2048]{2,0,1:T(8,128)S(1)}, f32[128,3,2048]{2,0,1:T(8,128)}, u32[]{:S(2)}) copy-start(f32[128,3,2048]{2,0,1:T(8,128)} %param.41) | copy-start | bytes 9437188
  571.0 32.6 %copy-start.8 = (bf16[3,64,4096]{2,1,0:T(8,128)(2,1)S(1)}, bf16[3,64,4096]{2,1,0:T(8,128)(2,1)}, u32[]{:S(2)}) copy-start(bf16[3,64,4096]{2,1,0:T(8,128)(2,1)} %get-tuple-element.136) | copy-start | bytes 4718596
  615.1 9.5 %copy-start = (f32[64,3,8192]{2,0,1:T(8,128)}, f32[64,3,8192]{2,0,1:T(8,128)S(1)}, u32[]{:S(2)}) copy-start(f32[64,3,8192]{2,0,1:T(8,128)S(1)} %get-tuple-element.203) | copy-start | bytes 18874372
  (8 other events, 18.6 us)
Sparse Core Ops, SparseCore 0:
  136.8 130.4 all-gather.2

commit v2 on v1

--- a/solution.py
+++ b/solution.py
@@ -1288,14 +1288,14 @@
         sems = self.swap.at[k, n]
         return remote(part, self.theirs.at[k - 1, n], sems.at[0], sems.at[1], here.low_peer(k))
 
-    def begin(self):
+    def begin(self, start, stop):
         def one(n, carry):
             self.own_copy(n).start()
             for k in range(1, self.here.nl):
                 self.swap_copy(k, n).start()
             return carry
 
-        lax.fori_loop(0, self.here.groups, one, 0)
+        lax.fori_loop(start, stop, one, 0)
 
     def merged(self, n):
         self.own_copy(n).wait()
@@ -1375,7 +1375,7 @@
         to_far(k).start()
     if extras:
         column = Columns(here, extra_in[0], columns)
-        column.begin()
+        column.begin(0, here.groups)
     mine = total(here.z)
     for k in range(1, nz):
         to_far(k).wait_recv()
@@ -1473,8 +1473,8 @@
 def exit_kernel(
     dims, modes_ref, joint_ref, w_ref, ing_ref, dtg_ref, outg_ref, xg_ref, suma_ref, sumb_ref,
     x_ref, cot_ref, gain_ref, pick_ref,
-    grad_out, gsum_out, ing_out, dtg_out, outg_out, xg_out, suma_out, sumb_out,
-    part_ref, gparts, gslots, ready, pairs, smalls, cols, *bufs,
+    grad_out, gsum_out, ready_out, dtg_out, outg_out, xg_out, suma_out, sumb_out,
+    part_ref, gparts, gslots, pairs, smalls, *bufs,
 ):
     here = Place(dims)
     rows_d, chan = ing_ref.shape[3], ing_ref.shape[4]
@@ -1486,20 +1486,6 @@
     reduce = Reduce(here, part_ref, MBLK, bufs, False)
     column = Columns(here, ing_ref, columns)
 
-    def landing(g):
-        return ing_out.at[:, :, pl.ds(pl.multiple_of(g * chan, chan), chan)]
-
-    def col_copy(n, g):
-        return remote(ready.at[n], landing(g), cols.at[n, 0], cols.at[n, 1], here.of_group(here.after(n), here.l))
-
-    def own_copy():
-        return pltpu.make_async_copy(ready.at[0], landing(here.g), cols.at[0, 0])
-
-    def send_inner(n, carry):
-        ready[n] = column.merged(n)
-        col_copy(n, here.g).start()
-        return carry
-
     def pair_copies(k):
         to = here.low_after(k)
         peer = here.low_peer(k)
@@ -1524,22 +1510,24 @@
         lax.fori_loop(0, plane, one, 0)
         reduce.first(k)
 
-    first(0)
-    first(1)
-    column.begin()
+    for k in range(min(3, nz)):
+        first(k)
     for k in range(nz):
-        if k + 2 < nz:
-            first(k + 2)
-        if k == 1:
-            for low in range(1, here.nl):
-                for copy in pair_copies(low):
-                    copy.start()
+        if k + 3 < nz:
+            first(k + 3)
         reduce.second(k)
         if k > 0:
             reduce.third(k - 1)
-        lax.fori_loop(max(k * plane, 1), (k + 1) * plane, send_inner, 0)
-    ready[0] = column.merged(0)
-    own_copy().start()
+        column.begin(k * plane, (k + 1) * plane)
+    for low in range(1, here.nl):
+        for copy in pair_copies(low):
+            copy.start()
+
+    def merge(n, carry):
+        ready_out[here.after(n)] = column.merged(n)
+        return carry
+
+    lax.fori_loop(0, here.groups, merge, 0)
     reduce.last()
 
     acc = reduce.acc
@@ -1570,14 +1558,6 @@
     for k in range(1, here.nl):
         for copy in pair_copies(k):
             copy.wait()
-    own_copy().wait()
-
-    def end_cols(n, carry):
-        col_copy(n, here.before(n)).wait()
-        return carry
-
-    lax.fori_loop(1, here.groups, end_cols, 0)
-
     def end_small(k, carry):
         small_copy(k).wait()
         return carry
@@ -1594,16 +1574,15 @@
     return pl.pallas_call(
         functools.partial(exit_kernel, dims),
         in_specs=[pl.BlockSpec(memory_space=pltpu.SMEM)] + [vmem_spec()] * 2 + [any_spec()] * 6 + [vmem_spec()] * 4,
-        out_specs=[vmem_spec()] * 2 + [any_spec()] * 6,
+        out_specs=[vmem_spec()] * 3 + [any_spec()] * 5,
         out_shape=[
-            shape((MBLK, D), BF16), shape((8, 128), F32), shape((MODES, rows_d, INNER), BF16),
+            shape((MBLK, D), BF16), shape((8, 128), F32), shape((groups, MODES, rows_d, chan), BF16),
             *[shape((nl - 1, MODES) + part.shape[2:], F32) for part in swapped],
             *[shape((nl - 1, part.shape[-2], rows_e), F32) for part in rest],
         ],
         scratch_shapes=[
             VMEM((ns // NX, NX, ny, MBLK, D), BF16),
-            VMEM((D // 128, 8, 128), F32), VMEM((devices, 8, 128), F32), VMEM((groups, MODES, rows_d, chan), BF16),
-            DMA((nl, 5, 2)), DMA((devices, 2)), DMA((groups, 2)),
+            VMEM((D // 128, 8, 128), F32), VMEM((devices, 8, 128), F32), DMA((nl, 5, 2)), DMA((devices, 2)),
             *column_scratch(dims, rows_d, chan),
             *reduce_scratch(dims, MBLK, D, BF16),
         ],
@@ -1660,6 +1639,7 @@
     scanned, mixed, before, last, *out_parts = forward_scan(
         plan, jnp.concatenate([modes, spot]), proj, act, gate, w_dt, w_out, par, rates_f, select
     )
+    cot, out_parts = lax.optimization_barrier((cot, out_parts))
     staged = Staged(dims, out_parts)
     crossed = staged.plane()
 
@@ -1673,23 +1653,28 @@
     bproj, gate_ready = share(dims, 3, bproj_part, (gate_g,))
     bproj = bproj.reshape(groups, XCOLS, MBLK)
     gate_grad = lax.all_to_all(gate_ready, GROUP, 0, 0)
+    crossed, bproj = lax.optimization_barrier((crossed, bproj))
+    pieces = staged.along(staged.line(crossed))
     joint, in_g, x_g, sums_b = tail(
         plan, modes, bproj, bact, bgate, pre, act, inner, normal, w_x, par
     )
     rest = (x_g.reshape(MODES * XCOLS, chan), sums_a, sums_b)
-    input_grad, gain_sum, inner_grad, dt_far, out_far, *rest_far = leave(
+    input_grad, gain_sum, inner_ready, dt_far, out_far, *rest_far = leave(
         dims, modes, joint, w_in, in_g.reshape(MODES, groups, los, rows_d, chan), (dt_g, out_g),
         tuple(lanes_split(part, los) for part in rest), tokens[0], cotangent[0], gain, pick,
     )
 
-    crossed, gain_sum = lax.optimization_barrier((crossed, gain_sum))
-    pieces = staged.along(staged.line(crossed))
+    inner_ready, gate_grad, pieces, gain_sum, dt_far, out_far, rest_far = lax.optimization_barrier(
+        (inner_ready, gate_grad, pieces, gain_sum, dt_far, out_far, rest_far)
+    )
+    inner_grad = lax.all_to_all(inner_ready, GROUP, 0, 0)
 
     def merged(near, far):
         return lax.dynamic_index_in_dim(near, low, 1, keepdims=False) + jnp.sum(far, 0)
 
-    gate_grad = gate_grad.transpose(2, 1, 0, 3).reshape(rows_d, MODES, INNER)
-    in_grad = jnp.concatenate([inner_grad.swapaxes(0, 1), gate_grad], 2).astype(F32)
+    in_grad = jnp.concatenate(
+        [half.transpose(2, 1, 0, 3).reshape(rows_d, MODES, INNER) for half in (inner_grad, gate_grad)], 2
+    ).astype(F32)
     dt_grad = merged(dt_g, dt_far).swapaxes(0, 1)
     out_grad = merged(out_g, out_far).swapaxes(0, 1)
     x_sum, sum_a, sum_b = (
@@ -1714,7 +1699,6 @@
     out_new = adam_update(out_weight, out_first, out_second, out_grad, (4 * INNER) ** (-0.5))
     gain_new = adam_update(norm_gain, gain_first, gain_second, gain_grad, SMALL_RATE)
     chan_new = adam_update(channel_params, chan_first, chan_second, chan_grad, CHAN_RATE)
-    pieces, in_new = lax.optimization_barrier((pieces, in_new))
     out_sum = tokens[0].astype(F32)
     for piece in pieces:
         out_sum = out_sum + piece.astype(F32)

time: 636 us -> 609 us (0.958)
  Pallas kernels: 476 us -> 457 us
  waiting for transfers between devices: 71.1 us -> 59.1 us
    all_to_all x1, waiting for transfers between devices: 31 us -> 0.01 us  [body(): gate_grad = lax.all_to_all(gate_ready, GROUP, 0, 0)]
    pallas_call x1, Pallas kernels: 144 us -> 125 us  [leave(): pl.pallas_call(functools.partial(exit_kernel, dims), in_specs=[pl.BlockSp...]
    all_to_all x0 -> x1, waiting for transfers between devices: none -> 17 us  [body(): inner_grad = lax.all_to_all(inner_ready, GROUP, 0, 0)]
    ppermute x3, waiting for transfers between devices: 0.01 us -> 15.9 us  [plane(): out.append(lax.ppermute(self.parts[r], GROUP, moves))]
    convert_element_type x1, other arithmetic: 2.06 us -> 13.8 us  [body(): in_new[0].astype(BF16)]
    add x1 -> x0, other arithmetic: 11.4 us -> none  [adam_update(): second_new = BETA_TWO * second + (1.0 - BETA_TWO) * grad * grad]
    ppermute x3, waiting for transfers between devices: 7.47 us -> 0.01 us  [along(): out.append(lax.ppermute(piece, 'seq', moves))]
    all_gather x1, waiting for transfers between devices: 32.6 us -> 26.2 us  [body(): cot = lax.all_gather(cot_here, GROUP, axis=0)]
  transfers between devices with their start and end apart: 8 -> 9, of which waited for: 4 -> 3; matrix products, arithmetic and copies ran while one was open for 6% -> 5% of each run, Pallas kernels for 26% -> 51%
where the time goes in v2:
time: 609 us; the launch traced here: 608 us
  Pallas kernels  457 us (75%)
  waiting for transfers between devices  59.1 us (10%)
  other arithmetic  51.6 us (8%)
  starting transfers between devices  18.3 us (3%)
  between operations  15.1 us (2%)
  local copies, waits for them, and re-layouts  6.46 us (1%)
    pallas_call x1, Pallas kernels, leave(): pl.pallas_call(functools.partial(exit_kernel, dims), in_specs=[pl.BlockSp...  125 us
    pallas_call x1, Pallas kernels, entry(): pl.pallas_call(functools.partial(entry_kernel, dims), in_specs=[vmem_spec...  118 us
    pallas_call x1, Pallas kernels, backward_scan(): pl.pallas_call(functools.partial(back_kernel, plan), grid_spec=pltpu.Pref...  73.3 us
    pallas_call x2, Pallas kernels, share(): pl.pallas_call(functools.partial(share_kernel, dims, len(extras)), in_spe...  71.4 us
    pallas_call x1, Pallas kernels, forward_scan(): pl.pallas_call(functools.partial(scan_kernel, plan), grid_spec=pltpu.Pref...  36.6 us
    all_gather x1, waiting for transfers between devices, body(): cot = lax.all_gather(cot_here, GROUP, axis=0)  26.2 us
    pallas_call x1, Pallas kernels, tail(): pl.pallas_call(functools.partial(tail_kernel, plan), grid_spec=pltpu.Pref...  17.6 us
    all_to_all x1, waiting for transfers between devices, body(): inner_grad = lax.all_to_all(inner_ready, GROUP, 0, 0)  17 us
  transfers between devices with their start and end apart: 9, of which 3 were waited for; matrix products, arithmetic and copies ran while one was open for 5% of the time, Pallas kernels for 51%

profile of v2, /device:TPU:10, one launch (start us, length us, event | category | flops | bytes accessed | tf_op | source)
XLA Modules:
  0.0 607.9 jit_solution(3759363804890520325)
XLA Ops:
  9.2 5.0 convert_bitcast_fusion.win_ref
  18.5 118.1 %entry.1 = (f32[8,128]{1,0:T(8,128)}, f32[8,2048]{1,0:T(8,128)}, bf16[16,128,2048]{2,1,0:T(8,128)(2,1)}, bf16[3,2048,512]{2,1,0:T(8,128)(2,1)}, bf16[3,256,128]{...) custom-call(f32[8,128]{1,0:T(8,128)} %copy-done.17, ...), custom_call_target="tpu_custom_call" | custom-call | bytes 300000000 | tf_op jit(solution)/shard_map/entry/pallas_call | solution.py:1251
  137.8 15.4 %front.1 = (bf16[16,128,256]{2,1,0:T(8,128)(2,1)}, f32[16,128,256]{2,1,0:T(8,128)}, f32[16,128,256]{2,1,0:T(8,128)}, bf16[16,128,256]{2,1,0:T(8,128)(2,1)}, bf16[16,160,128]{2,1,0:T(8,128)(2,1)}) custom-call(s32[16]{0:T(128)} %convert_bitcast_fusion.3.modes.modes_ref, bf16[16,128,2048]{2,1,0:T(8,128)(2,1)} %get-tuple-element.107.x_ref, ...), custom_call_target="tpu_custom_call" | custom-call | flops 4294967296 | bytes 25165824 | tf_op jit(solution)/shard_map/front/pallas_call | solution.py:184
  153.3 39.9 %share.2 = bf16[4,4,160,128]{3,2,1,0:T(8,128)(2,1)} custom-call(bf16[4,4,160,128]{3,2,1,0:T(8,128)(2,1)} %bitcast.131), custom_call_target="tpu_custom_call" | custom-call | bytes 90000000 | tf_op jit(solution)/shard_map/share/pallas_call | solution.py:1423
  194.5 36.6 %forward_scan.1 = (f32[16,128,256]{2,1,0:T(8,128)}, bf16[16,128,256]{2,1,0:T(8,128)(2,1)}, f32[1024,8,8,128]{3,2,1,0:T(8,128)}, f32[8,8,128]{2,1,0:T(8,128)}, bf...) custom-call(s32[18]{0:T(128)} %pad_add_fusion.modes, ...), custom_call_target="tpu_custom_call" | custom-call | flops 503316480 | bytes 157286400 | tf_op jit(solution)/shard_map/forward_scan/pallas_call | solution.py:299
  231.1 26.2 %all-gather.3.cloned.1.call-done = bf16[2048,2048]{1,0:T(8,128)(2,1)} async-done(((bf16[128,2048]{1,0:T(8,128)(2,1)}), bf16[2048,2048]{1,0:T(8,128)(2,1)}) %all-gather.3.cloned.1.call-update) | async-done | bytes 8388624 | tf_op jit(solution)/shard_map/all_gather | solution.py:1633
  260.8 73.3 %backward_scan.1 = (f32[16,128,256]{2,1,0:T(8,128)}, bf16[16,128,256]{2,1,0:T(8,128)(2,1)}, bf16[16,160,128]{2,1,0:T(8,128)(2,1)}, f32[3,256,128]{2,1,0:T(8,128)...) custom-call(s32[16]{0:T(128)} %convert_bitcast_fusion.3.modes.modes_ref, ...), custom_call_target="tpu_custom_call" | custom-call | flops 838860800 | bytes 314572800 | tf_op jit(solution)/shard_map/backward_scan/pallas_call | solution.py:488
  334.1 15.9 %collective-permute-done.2 = bf16[4,128,2048]{2,1,0:T(8,128)(2,1)} collective-permute-done((bf16[4,128,2048]{2,1,0:T(8,128)(2,1)}, bf16[4,128,2048]{2,1,0:T(8,128)(2,1)}, u32[]{:S(2)}, u32[]{:S(2)}) %collective-permute-start.2) | collective-permute-done | bytes 2097184 | tf_op jit(solution)/shard_map/ppermute | solution.py:1455
  350.0 31.5 %share.3 = (bf16[4,4,160,128]{3,2,1,0:T(8,128)(2,1)}, bf16[16,3,64,256]{3,2,1,0:T(8,128)(2,1)}) custom-call(bf16[4,4,160,128]{3,2,1,0:T(8,128)(2,1)} %bitcast.132, f32[3,16,2,64,256]{4,3,2,1,0:T(8,128)} %bitcast.118), custom_call_target="tpu_custom_call" | custom-call | bytes 90000000 | tf_op jit(solution)/shard_map/share/pallas_call | solution.py:1423
  381.5 5.5 all-to-all-start
  387.0 4.6 add_convert_fusion
  397.4 17.6 %tail.1 = (bf16[16,128,512]{2,1,0:T(8,128)(2,1)}, f32[3,2048,256]{2,1,0:T(8,128)}, f32[3,160,256]{2,1,0:T(8,128)}, f32[8,256]{1,0:T(8,128)}) custom-call(s32[16]{0:T(128)} %convert_bitcast_fusion.3.modes.modes_ref, bf16[16,160,128]{2,1,0:T(8,128)(2,1)} %bitcast.138, f32[16,128,256]{2,1,0:T(8,128)} %get-tuple-element.136.bact_ref, ...), custom_call_target="tpu_custom_call" | custom-call | flops 8589934592 | bytes 41943040 | tf_op jit(solution)/shard_map/tail/pallas_call | solution.py:579
  415.0 124.9 %leave.1 = (bf16[128,2048]{1,0:T(8,128)(2,1)}, f32[8,128]{1,0:T(8,128)}, bf16[16,3,64,256]{3,2,1,0:T(8,128)(2,1)}, f32[1,3,128,128]{3,2,1,0:T(8,128)}, f32[1,3,1...) custom-call(s32[16]{0:T(128)} %convert_bitcast_fusion.3.modes.modes_ref, ...), custom_call_target="tpu_custom_call" | custom-call | bytes 300000000 | tf_op jit(solution)/shard_map/leave/pallas_call | solution.py:1574
  541.4 1.7 bitcast_add_fusion.2
  543.1 4.9 all-to-all-start.1
  548.0 1.6 copy.53
  550.5 2.3 fusion.14
  553.6 1.8 broadcast_multiply_fusion.2
  555.4 2.3 fusion.16
  557.7 2.6 fusion.3
  560.3 6.8 %fusion.12 = (bf16[128,3,2048]{2,0,1:T(8,128)(2,1)}, f32[128,3,2048]{2,0,1:T(8,128)}, f32[128,3,2048]{2,0,1:T(8,128)}, f32[3,128,2048]{2,1,0:T(8,128)S(1)}) fusion(f32[128,3,2048]{2,0,1:T(8,128)S(1)} %copy-done.1, f32[128,3,2048]{2,0,1:T(8,128)S(1)} %copy-done.2, f32[128,3,2048]{2,0,1:T(8,128)} %param.42, f32[1,3,128,2048]{3,2,1,0:T(8,128)} %get-tuple-element.168, ...), kind=kLoop, calls=%fused_computation.53 | loop fusion | flops 11796480 | bytes 26738692 | tf_op jit(solution)/shard_map/convert_element_type | solution.py:1716
  567.1 2.2 broadcast_multiply_fusion
  569.3 17.0 %all-to-all-done.1 = bf16[16,3,64,256]{3,2,1,0:T(8,128)(2,1)S(1)} async-done(((bf16[16,3,64,256]{3,2,1,0:T(8,128)(2,1)}), bf16[16,3,64,256]{3,2,1,0:T(8,128)(2,1)S(1)}, u32[]{:S(2)}, u32[]{:S(2)}) %all-to-all-start.1) | async-done | bytes 1572896 | tf_op jit(solution)/shard_map/all_to_all | solution.py:1670
  586.5 13.8 %fusion.18 = (bf16[64,3,8192]{2,0,1:T(8,128)(2,1)}, f32[64,3,8192]{2,0,1:T(8,128)}, f32[64,3,8192]{2,0,1:T(8,128)}, f32[64,3,8192]{2,0,1:T(8,128)}) fusion(f32[64,3,8192]{2,0,1:T(8,128)} %param.29, f32[64,3,8192]{2,0,1:T(8,128)} %param.35, bf16[64,3,4096]{2,0,1:T(8,128)(2,1)S(1)} %bitcast.115, bf16[64,3,4096]{2,0,1:T(8,128)(2,1)S(1)} %bitcast.116, ...), kind=kLoop, calls=%fused_computation.56 | loop fusion | flops 29884416 | bytes 44040192 | tf_op jit(solution)/shard_map/convert_element_type | solution.py:1710
  (91 shorter events, 21.4 us)
Async XLA Ops:
  7.2 250.1 %all-gather.3.cloned.1.call-start = ((), (), s32[]{:S(2)}) async-start(), calls=%async_computation.2 | async-start | bytes 8912896 | tf_op jit(solution)/shard_map/all_gather | solution.py:1633
  9.2 5.0 copy-start
  137.8 55.3 %copy-start.11 = (f32[32,256]{1,0:T(8,128)S(1)}, f32[32,256]{1,0:T(8,128)}, u32[]{:S(2)}) copy-start(f32[32,256]{1,0:T(8,128)} %get-tuple-element.110.par_ref) | copy-start | bytes 98308
  137.8 55.4 %copy-start.19 = (s32[16]{0:T(128)S(1)}, s32[16]{0:T(128)}, u32[]{:S(2)}) copy-start(s32[16]{0:T(128)} %convert_bitcast_fusion.3.modes.modes_ref) | copy-start | bytes 196
  257.3 76.8 %collective-permute-start = (bf16[4,128,2048]{2,1,0:T(8,128)(2,1)}, bf16[4,128,2048]{2,1,0:T(8,128)(2,1)S(1)}, u32[]{:S(2)}, u32[]{:S(2)}) collective-permute-start(bf16[4,128,2048]{2,1,0:T(8,128)(2,1)} %get-tuple-element.120), channel_id=1, source_target_pairs={{0,2},{2,0},{4,6},{6,4},{8,10},{10,8},{12,14},{14,12},{16,18},{18,... | collective-permute-start | bytes 6291464 | tf_op jit(solution)/shard_map/ppermute | solution.py:1455
  258.1 76.0 %collective-permute-start.1 = (bf16[4,128,2048]{2,1,0:T(8,128)(2,1)}, bf16[4,128,2048]{2,1,0:T(8,128)(2,1)}, u32[]{:S(2)}, u32[]{:S(2)}) collective-permute-start(bf16[4,128,2048]{2,1,0:T(8,128)(2,1)} %get-tuple-element.121), channel_id=1, source_target_pairs={{0,4},{2,6},{4,0},{6,2},{8,12},{10,14},{12,8},{14,10},{16,20},{18,... | collective-permute-start | bytes 6291464 | tf_op jit(solution)/shard_map/ppermute | solution.py:1455
  259.5 90.5 %collective-permute-start.2 = (bf16[4,128,2048]{2,1,0:T(8,128)(2,1)}, bf16[4,128,2048]{2,1,0:T(8,128)(2,1)}, u32[]{:S(2)}, u32[]{:S(2)}) collective-permute-start(bf16[4,128,2048]{2,1,0:T(8,128)(2,1)} %get-tuple-element.122), channel_id=1, source_target_pairs={{0,6},{2,4},{4,2},{6,0},{8,14},{10,12},{12,10},{14,8},{16,22},{18,... | collective-permute-start | bytes 6291464 | tf_op jit(solution)/shard_map/ppermute | solution.py:1455
  334.1 15.9 %copy-start.5 = (bf16[4,128,2048]{2,1,0:T(8,128)(2,1)}, bf16[4,128,2048]{2,1,0:T(8,128)(2,1)S(1)}, u32[]{:S(2)}) copy-start(bf16[4,128,2048]{2,1,0:T(8,128)(2,1)S(1)} %collective-permute-done) | copy-start | bytes 6291460
  381.5 5.5 copy-start.4
  381.5 158.4 %all-to-all-start = ((bf16[16,3,64,256]{3,2,1,0:T(8,128)(2,1)}), bf16[16,3,64,256]{3,2,1,0:T(8,128)(2,1)}, u32[]{:S(2)}, u32[]{:S(2)}) async-start(bf16[16,3,64,256]{3,2,1,0:T(8,128)(2,1)} %get-tuple-element.148), calls=%async_computation | async-start | bytes 3145728 | tf_op jit(solution)/shard_map/all_to_all | solution.py:1655
  393.0 146.9 %collective-permute-start.3 = (bf16[128,2048]{1,0:T(8,128)(2,1)}, bf16[128,2048]{1,0:T(8,128)(2,1)}, u32[]{:S(2)}, u32[]{:S(2)}) collective-permute-start(bf16[128,2048]{1,0:T(8,128)(2,1)} %get-tuple-element.193), channel_id=1, source_target_pairs={{0,8},{4,12},{8,16},{12,20},{16,24},{20,28},{24,0},{28,4},{1,9},{5... | collective-permute-start | bytes 1572872 | tf_op jit(solution)/shard_map/ppermute | solution.py:1469
  394.4 145.5 %collective-permute-start.4 = (bf16[128,2048]{1,0:T(8,128)(2,1)}, bf16[128,2048]{1,0:T(8,128)(2,1)}, u32[]{:S(2)}, u32[]{:S(2)}) collective-permute-start(bf16[128,2048]{1,0:T(8,128)(2,1)} %get-tuple-element.192), channel_id=1, source_target_pairs={{0,16},{4,20},{8,24},{12,28},{16,0},{20,4},{24,8},{28,12},{1,17},{... | collective-permute-start | bytes 1572872 | tf_op jit(solution)/shard_map/ppermute | solution.py:1469
  395.9 144.0 %collective-permute-start.5 = (bf16[128,2048]{1,0:T(8,128)(2,1)}, bf16[128,2048]{1,0:T(8,128)(2,1)}, u32[]{:S(2)}, u32[]{:S(2)}) collective-permute-start(bf16[128,2048]{1,0:T(8,128)(2,1)} %get-tuple-element.191), channel_id=1, source_target_pairs={{0,24},{4,28},{8,0},{12,4},{16,8},{20,12},{24,16},{28,20},{1,25},{... | collective-permute-start | bytes 1572872 | tf_op jit(solution)/shard_map/ppermute | solution.py:1469
  415.0 125.0 %copy-start.14 = (f32[8,256]{1,0:T(8,128)S(1)}, f32[8,256]{1,0:T(8,128)}, u32[]{:S(2)}) copy-start(f32[8,256]{1,0:T(8,128)} %get-tuple-element.146.sumb_ref) | copy-start | bytes 24580
  415.0 125.7 %copy-start.13 = (f32[24,256]{1,0:T(8,128)S(1)}, f32[24,256]{1,0:T(8,128)}, u32[]{:S(2)}) copy-start(f32[24,256]{1,0:T(8,128)} %get-tuple-element.145.suma_ref) | copy-start | bytes 73732
  415.0 126.4 %copy-start.7 = (f32[3,160,256]{2,1,0:T(8,128)S(1)}, f32[3,160,256]{2,1,0:T(8,128)}, u32[]{:S(2)}) copy-start(f32[3,160,256]{2,1,0:T(8,128)} %get-tuple-element.144) | copy-start | bytes 1474564
  543.1 6.8 %copy-start.15 = (f32[128,25]{0,1:T(8,128)S(1)}, f32[128,25]{0,1:T(8,128)}, u32[]{:S(2)}) copy-start(f32[128,25]{0,1:T(8,128)} %param.45) | copy-start | bytes 38404
  543.1 6.8 %copy-start.16 = (f32[128,25]{0,1:T(8,128)S(1)}, f32[128,25]{0,1:T(8,128)}, u32[]{:S(2)}) copy-start(f32[128,25]{0,1:T(8,128)} %param.46) | copy-start | bytes 38404
  543.1 43.3 %all-to-all-start.1 = ((bf16[16,3,64,256]{3,2,1,0:T(8,128)(2,1)}), bf16[16,3,64,256]{3,2,1,0:T(8,128)(2,1)S(1)}, u32[]{:S(2)}, u32[]{:S(2)}) async-start(bf16[16,3,64,256]{3,2,1,0:T(8,128)(2,1)} %get-tuple-element.164), calls=%async_computation.1 | async-start | bytes 3145728 | tf_op jit(solution)/shard_map/all_to_all | solution.py:1670
  549.9 7.8 %copy-start.3 = (bf16[1,128,2048]{2,1,0:T(8,128)(2,1)S(1)}, bf16[1,128,2048]{2,1,0:T(8,128)(2,1)}, u32[]{:S(2)}) copy-start(bf16[1,128,2048]{2,1,0:T(8,128)(2,1)} %param.26) | copy-start | bytes 1572868
  549.9 7.8 %copy-start.6 = (bf16[128,2048]{1,0:T(8,128)(2,1)S(1)}, bf16[128,2048]{1,0:T(8,128)(2,1)}, u32[]{:S(2)}) copy-start(bf16[128,2048]{1,0:T(8,128)(2,1)} %get-tuple-element.159) | copy-start | bytes 1572868
  550.5 9.7 %copy-start.2 = (f32[128,3,2048]{2,0,1:T(8,128)S(1)}, f32[128,3,2048]{2,0,1:T(8,128)}, u32[]{:S(2)}) copy-start(f32[128,3,2048]{2,0,1:T(8,128)} %param.41) | copy-start | bytes 9437188
  552.9 7.4 %copy-start.1 = (f32[128,3,2048]{2,0,1:T(8,128)S(1)}, f32[128,3,2048]{2,0,1:T(8,128)}, u32[]{:S(2)}) copy-start(f32[128,3,2048]{2,0,1:T(8,128)} %param.32) | copy-start | bytes 9437188
  586.5 13.8 %copy-start.10 = (bf16[128,2048]{1,0:T(8,128)(2,1)S(1)}, bf16[128,2048]{1,0:T(8,128)(2,1)}, u32[]{:S(2)}) copy-start(bf16[128,2048]{1,0:T(8,128)(2,1)} %get-tuple-element.163) | copy-start | bytes 1572868
  (8 other events, 26.4 us)
Sparse Core Ops, SparseCore 0:
  136.8 120.5 all-gather.2
